TPU v7x, 512 devices: a whole 4x4x16 slice. The times are simulated.
512 devices in a mesh: wide: 128 (over z, x, y_lo), narrow: 4 (over y_hi, core).
Axes of the slice: x: 4, y: 4 (y_hi: 2, y_lo: 2; y = y_hi * 2 + y_lo), z: 16, core: 2. Of those that a mesh axis runs over, the one named last changes fastest.
Arguments:
- star_pos: float32 [3, 32768], P(None, ('wide', 'narrow')), may hold values from -6 to 6
- star_vel: float32 [3, 32768], P(None, ('wide', 'narrow')), may hold values from -6 to 6
- star_mass: float32 [32768], P(('wide', 'narrow')), may hold values from 0.00048828125 to 0.0048828125
- star_acc: float32 [3, 32768], P(None, ('wide', 'narrow')), may hold values from -6 to 6
- star_jerk: float32 [3, 32768], P(None, ('wide', 'narrow')), may hold values from -120 to 120
- gal_pos: float32 [3, 262144], P(None, ('wide', 'narrow')), may hold values from -6 to 6
- gal_vel: float32 [3, 262144], P(None, ('wide', 'narrow')), may hold values from -6 to 6
- gal_mass: float32 [262144], P(('wide', 'narrow')), may hold values from 0.0009765625 to 0.009765625
- group_of: int32 [262144], P(('wide', 'narrow')), may hold values from 0 to 31, as said below
- let_send: int32 [512, 128, 1], P(('wide', 'narrow')), may hold values from -1 to 3, as said below
- star_leaf: int32 [2048, 8], P(('wide', 'narrow')), may hold values from 0 to 127, as said below
Outputs:
- gal_vel_new: float32 [3, 262144], P(None, ('wide', 'narrow'))
- star_pos_new: float32 [3, 32768], P(None, ('wide', 'narrow'))
- star_vel_new: float32 [3, 32768], P(None, ('wide', 'narrow'))
Inputs may be any that keep to these rules, and one draw needn't show every extreme that they name: `group_of`: within each leaf of 128 bodies every group number is held by exactly 4 bodies. `let_send`: entry [k, j, s] is a local leaf of device k sent to the device of wide index j with k's narrow index, or -1 for an empty slot; the leaves of one row are distinct; a device lists nothing for its own wide index; for some wide index j, every device whose wide index is not j lists a leaf for j, in every draw. `star_leaf`: the star blocks listed for one leaf are distinct.
All inputs are finite; a program needn't handle non-finite values.
Results may differ from a plain program's by a relative error of at most 0.0003.
Values sent between devices are 32-bit elements; how exact they have to be, the bound alone decides.
No kernel may reach another device: no remote copies, remote signals or barrier semaphores. Data moves between devices by JAX's collectives and lax.ppermute only.
A program may use at most 64 MiB of HBM per device.

v0:
```python
import math

import jax
import jax.numpy as jnp
from jax import lax
from jax.sharding import Mesh
from jax.sharding import PartitionSpec as P

GROUPS = 32
WIDE = ("wide_0", "wide_1", "wide_2")
WIDE_NARROW = ("wide_0", "wide_1", "wide_2", "narrow")


time_step = 0.25
soften_sq = 0.05


def in_order(parts, dim):
    parts = jnp.moveaxis(parts, 0, dim)
    lengths = parts.shape
    return parts.reshape(*lengths[:dim], lengths[dim] * lengths[dim + 1], *lengths[dim + 2 :])


def stacked_from(x, axes, turns):
    parts = x[None]
    for k in turns:
        parts = lax.all_gather(parts, axes[k], axis=0, tiled=True)
    block = [lax.axis_size(axes[k]) for k in reversed(turns)]
    parts = parts.reshape(*block, *x.shape)
    turned = sorted(range(len(turns)), key=lambda place: turns[len(turns) - 1 - place])
    return parts.transpose(*turned, *range(len(turns), parts.ndim)).reshape(-1, *x.shape)


def whole_of(x, axes, turns, dim):
    return in_order(stacked_from(x, axes, turns), dim)


def cut_along(x, dim, size):
    lengths = x.shape
    parts = x.reshape(*lengths[:dim], size, lengths[dim] // size, *lengths[dim + 1 :])
    return jnp.moveaxis(parts, dim, 0)


def sum_at_owner(x, axis, dim):
    parts = cut_along(x, dim, lax.axis_size(axis))
    arrived = lax.all_to_all(parts, axis, split_axis=0, concat_axis=0, tiled=True)
    return arrived.sum(axis=0)


def by_blocks(kernel, arrays):
    total_rows = arrays[0].shape[1]
    block_rows = math.gcd(total_rows, 512)
    nblocks = total_rows // block_rows
    split = tuple(
        (
            member.reshape(member.shape[0], nblocks, block_rows).transpose(1, 0, 2)
            for member in arrays
        )
    )
    result = lax.map(kernel, split)
    return jax.tree.map(
        lambda piece: piece.transpose(1, 0, 2).reshape(piece.shape[1], total_rows), result
    )


def attract(tgt_pos, src_pos, src_mass):

    def kernel(pieces):
        here_pos = pieces[0]
        offset = src_pos[:, None, :] - here_pos[:, :, None]
        dist_sq = jnp.sum(offset * offset, axis=0) + soften_sq
        inverse = lax.rsqrt(dist_sq)
        weight = src_mass[None, :] * inverse * inverse * inverse
        return jnp.sum(offset * weight[None], axis=2)

    return by_blocks(kernel, (tgt_pos,))


def hermite(tgt_pos, tgt_vel, src_pos, src_vel, src_mass):

    def kernel(pieces):
        here_pos, here_vel = pieces
        offset = src_pos[:, None, :] - here_pos[:, :, None]
        rel_vel = src_vel[:, None, :] - here_vel[:, :, None]
        dist_sq = jnp.sum(offset * offset, axis=0) + soften_sq
        inverse = lax.rsqrt(dist_sq)
        weight = src_mass[None, :] * inverse * inverse * inverse
        approach = 3.0 * jnp.sum(offset * rel_vel, axis=0) / dist_sq
        accel_sum = jnp.sum(offset * weight[None], axis=2)
        jerk_sum = jnp.sum((rel_vel - offset * approach[None]) * weight[None], axis=2)
        return (accel_sum, jerk_sum)

    return by_blocks(kernel, (tgt_pos, tgt_vel))


def body(
    star_pos,
    star_vel,
    star_mass,
    star_acc,
    star_jerk,
    gal_pos,
    gal_vel,
    gal_mass,
    group_of,
    let_send,
    star_leaf,
):
    n_wide = lax.axis_size(WIDE)
    own_count = star_pos.shape[1]
    leaves = star_leaf.shape[0]
    leaf_size = gal_pos.shape[1] // leaves
    groups_per = GROUPS
    step_sq = time_step * time_step
    pred_pos = (
        star_pos
        + time_step * star_vel
        + step_sq * 0.5 * star_acc
        + step_sq * time_step / 6.0 * star_jerk
    )
    pred_vel = star_vel + time_step * star_acc + step_sq * 0.5 * star_jerk
    own_state = jnp.concatenate([pred_pos, pred_vel, star_mass[None]], axis=0)
    sibling = lax.all_gather(own_state, "narrow", axis=1, tiled=True)
    columns = whole_of(own_state, WIDE, (2, 0, 1), 1)
    onehot = (
        group_of.reshape(leaves, 1, leaf_size)
        == jnp.arange(groups_per, dtype=jnp.int32)[None, :, None]
    ).astype(jnp.float32)
    leaf_mass = gal_mass.reshape(leaves, leaf_size)
    leaf_pos = gal_pos.reshape(3, leaves, leaf_size)
    cell_mass = jnp.einsum("lgb,lb->lg", onehot, leaf_mass, precision=lax.Precision.HIGHEST)
    cell_mom = jnp.einsum(
        "lgb,clb->clg", onehot, leaf_pos * leaf_mass[None], precision=lax.Precision.HIGHEST
    )
    cells = jnp.concatenate([cell_mom / cell_mass[None], cell_mass[None]], axis=0)
    slot_ids = let_send[0]
    chosen = (slot_ids[:, :, None] == jnp.arange(leaves, dtype=jnp.int32)[None, None, :]).astype(
        jnp.float32
    )
    outgoing = jnp.einsum("wsl,clg->wcsg", chosen, cells, precision=lax.Precision.HIGHEST)
    outgoing = outgoing.reshape(n_wide, 4, slot_ids.shape[1] * groups_per)
    received = lax.all_to_all(outgoing, WIDE, split_axis=0, concat_axis=0, tiled=True)
    essential = received.transpose(1, 0, 2).reshape(4, -1)
    local_cells = cells.reshape(4, leaves * groups_per)
    accel_part, jerk_part = hermite(
        sibling[0:3], sibling[3:6], columns[0:3], columns[3:6], columns[6]
    )
    summed = sum_at_owner(jnp.concatenate([accel_part, jerk_part], axis=0), "narrow", 1)
    gal_acc = attract(gal_pos, gal_pos, gal_mass) + attract(gal_pos, essential[0:3], essential[3])
    picked = jnp.take(columns.reshape(7, n_wide, own_count), star_leaf, axis=1)
    picked = picked.reshape(7, leaves, star_leaf.shape[1] * own_count)
    star_term = jax.vmap(
        lambda target, source: attract(target, source[0:3], source[6]), in_axes=(1, 1), out_axes=1
    )(leaf_pos, picked)
    gal_acc = gal_acc + star_term.reshape(3, leaves * leaf_size)
    gal_vel_new = gal_vel + time_step * gal_acc
    all_cells = jnp.concatenate([local_cells, essential], axis=1)
    cell_acc = attract(pred_pos, all_cells[0:3], all_cells[3])
    new_acc = summed[0:3] + cell_acc
    new_jerk = summed[3:6]
    star_vel_new = (
        star_vel + time_step * 0.5 * (star_acc + new_acc) + step_sq / 12.0 * (star_jerk - new_jerk)
    )
    star_pos_new = (
        star_pos
        + time_step * 0.5 * (star_vel + star_vel_new)
        + step_sq / 12.0 * (star_acc - new_acc)
    )
    return (gal_vel_new, star_pos_new, star_vel_new)


def solution(mesh):
    torus = Mesh(
        mesh.devices.reshape(16, 4, 2, mesh.shape["narrow"]),
        ("wide_0", "wide_1", "wide_2", "narrow"),
    )
    return jax.shard_map(
        body,
        mesh=torus,
        in_specs=(
            P(None, WIDE_NARROW),
            P(None, WIDE_NARROW),
            P(WIDE_NARROW),
            P(None, WIDE_NARROW),
            P(None, WIDE_NARROW),
            P(None, WIDE_NARROW),
            P(None, WIDE_NARROW),
            P(WIDE_NARROW),
            P(WIDE_NARROW),
            P(WIDE_NARROW, None, None),
            P(WIDE_NARROW, None),
        ),
        out_specs=(P(None, WIDE_NARROW), P(None, WIDE_NARROW), P(None, WIDE_NARROW)),
        check_vma=False,
    )
```

profile of v0, /device:TPU:1, one launch (start us, length us, event | category | flops | bytes accessed | tf_op | source)
XLA Modules:
  0.0 153.7 jit_solution(15518168542261853254)
XLA Ops:
  0.6 0.7 multiply_add_fusion.3
  1.4 0.7 fusion.22
  2.0 3.8 %all-gather.1 = f32[2,7,64]{2,1,0:T(8,128)S(1)} all-gather(f32[1,7,64]{2,1,0:T(8,128)S(1)} %get-tuple-element.92), channel_id=2, replica_groups=mesh['wide_0'=16,'wide_1'=4,'wide_2'=2,'narrow'=4] {'wide_2'}, dimensions={0}, use_global_device_ids=true | all-gather | bytes 5376 | tf_op jit(solution)/shard_map/all_gather | solution.py:27
  5.8 29.0 %all_gather.13 = f32[32,7,64]{2,1,0:T(8,128)S(1)} all-gather(f32[2,7,64]{2,1,0:T(8,128)S(1)} %all-gather.1), channel_id=1, replica_groups=mesh['wide_0'=16,'wide_1'=4,'wide_2'=2,'narrow'=4] {'wide_0'}, dimensions={0}, use_global_device_ids=true | all-gather | bytes 60928 | tf_op jit(solution)/shard_map/all_gather | solution.py:27
  34.9 10.1 %all_gather.14 = f32[128,7,64]{2,0,1:T(8,128)S(1)} all-gather(f32[32,7,64]{2,0,1:T(8,128)S(1)} %copy.83), channel_id=1, replica_groups=mesh['wide_0'=16,'wide_1'=4,'wide_2'=2,'narrow'=4] {'wide_1'}, dimensions={0}, use_global_device_ids=true | all-gather | bytes 286720 | tf_op jit(solution)/shard_map/all_gather | solution.py:27
  45.8 18.4 %all-gather.2 = f32[4,64,7]{1,2,0:T(8,128)S(1)} all-gather(f32[1,64,7]{1,2,0:T(8,128)S(1)} %get-tuple-element.86), channel_id=1, replica_groups=mesh['wide_0'=16,'wide_1'=4,'wide_2'=2,'narrow'=4] {'narrow'}, dimensions={0}, use_global_device_ids=true | all-gather | bytes 8960 | tf_op jit(solution)/shard_map/all_gather | solution.py:123
  64.7 17.3 %fusion.4 = (f32[256,8192]{1,0:T(8,128)}, f32[256,8192]{1,0:T(8,128)}) fusion(f32[3,256]{1,0:T(4,128)S(1)} %get-tuple-element.83, f32[3,8192]{1,0:T(4,128)S(1)} %sub.146, f32[3,256]{1,0:T(4,128)S(1)} %get-tuple-element.82, f32[3,8192]{1,0:T(4,128)S(1)} %sub.150), kind=kLoop, calls=%fused_computation.12 | loop fusion | flops 33554432 | bytes 16979968 | tf_op jit(solution)/shard_map/while/body/eval_jaxpr/reduce_sum | solution.py:85
  82.0 7.0 %multiply_divide_fusion = (f32[256,8192]{1,0:T(8,128)S(1)}, f32[256,8192]{1,0:T(8,128)S(1)}) fusion(f32[256,8192]{1,0:T(8,128)} %get-tuple-element.65, f32[256,8192]{1,0:T(8,128)} %get-tuple-element.64, f32[8192]{0:T(1024)S(1)} %mul.357), kind=kLoop, calls=%fused_computation.17 | loop fusion | flops 12582912 | bytes 33587200 | tf_op jit(solution)/shard_map/while/body/eval_jaxpr/div | solution.py:88
  89.0 12.2 %fusion.5 = (f32[3,256]{1,0:T(4,128)S(1)}, f32[3,256]{1,0:T(4,128)S(1)}) fusion(f32[256,8192]{1,0:T(8,128)S(1)} %get-tuple-element.74, f32[3,256]{1,0:T(4,128)S(1)} %get-tuple-element.83, f32[3,8192]{1,0:T(4,128)S(1)} %sub.146, f32[256,8192]{1,0:T(8,128)S(1)} %get-tuple-element.73, f32[3,256]{1,0:T(4,128)S(1)} %get-tuple-element.82, f32[3,8192]{1,0:T(4,128)S(1)} %sub.150), kind=kLoop, calls=%fused_computation.13 | loop fusion | flops 50330112 | bytes 16986112 | tf_op jit(solution)/shard_map/while/body/eval_jaxpr/reduce_sum | solution.py:89
  101.3 0.7 reshape.253
  102.0 4.7 %all-to-all-start.1 = ((f32[4,1,384]{2,1,0:T(1,128)}), f32[4,1,384]{2,1,0:T(1,128)S(1)}, u32[]{:S(2)}, u32[]{:S(2)}) async-start(f32[4,1,384]{2,1,0:T(1,128)} %reshape.253), calls=%async_computation.1 | async-start | bytes 12288 | tf_op jit(solution)/shard_map/all_to_all | solution.py:46
  106.8 0.6 gather_fusion
  109.7 0.8 reshape.251
  110.5 0.8 all-to-all-done.1
  111.3 10.7 %all-to-all-start = ((f32[128,1,128]{2,1,0:T(1,128)}), f32[128,1,128]{2,1,0:T(1,128)S(1)}, u32[]{:S(2)}, u32[]{:S(2)}) async-start(f32[128,1,128]{2,1,0:T(1,128)} %reshape.251), calls=%async_computation | async-start | bytes 131072 | tf_op jit(solution)/shard_map/all_to_all | solution.py:142
  122.8 0.7 fusion.12
  123.9 0.7 reduce.11
  124.7 10.6 %all-to-all-done = f32[128,1,128]{2,1,0:T(1,128)S(1)} async-done(((f32[128,1,128]{2,1,0:T(1,128)}), f32[128,1,128]{2,1,0:T(1,128)S(1)}, u32[]{:S(2)}, u32[]{:S(2)}) %all-to-all-start) | async-done | bytes 65568 | tf_op jit(solution)/shard_map/all_to_all | solution.py:142
  135.3 0.8 reduce.10
  138.2 3.2 %fusion = f32[512,4096]{1,0:T(8,128)S(1)} fusion(f32[3,512]{1,0:T(4,128)S(1)} %copy-done, f32[3,4096]{1,0:T(4,128)S(1)} %sub.139), kind=kLoop, calls=%fused_computation.8 | loop fusion | flops 16777216 | bytes 8443904 | tf_op jit(solution)/shard_map/while/body/eval_jaxpr/reduce_sum | solution.py:71
  141.4 4.9 %multiply_multiply_fusion.1 = f32[512,4096]{1,0:T(8,128)} fusion(f32[512,4096]{1,0:T(8,128)S(1)} %fusion, f32[4096]{0:T(1024)S(1)} %mul.333), kind=kLoop, calls=%fused_computation.16 | loop fusion | flops 8388608 | bytes 16793600 | tf_op jit(solution)/shard_map/while/body/eval_jaxpr/mul | solution.py:73
  146.4 6.1 %fusion.1 = f32[3,512]{1,0:T(4,128)S(1)} fusion(f32[512,4096]{1,0:T(8,128)} %multiply_multiply_fusion.1, f32[3,512]{1,0:T(4,128)S(1)} %copy-done, f32[3,4096]{1,0:T(4,128)S(1)} %sub.139), kind=kLoop, calls=%fused_computation.9 | loop fusion | flops 18872832 | bytes 8450048 | tf_op jit(solution)/shard_map/while/body/eval_jaxpr/reduce_sum | solution.py:74
  152.5 0.6 multiply_add_fusion
  153.1 0.6 fusion.19
  (77 shorter events, 7.0 us)
Async XLA Ops:
  88.9 17.8 %copy-start.2 = (s32[4,8]{1,0:T(4,128)S(1)}, s32[4,8]{1,0:T(4,128)}, u32[]{:S(2)}) copy-start(s32[4,8]{1,0:T(4,128)} %param.21) | copy-start | bytes 388
  88.9 18.6 %copy-start = (f32[3,512]{1,0:T(4,128)S(1)}, f32[3,512]{1,0:T(4,128)}, u32[]{:S(2)}) copy-start(f32[3,512]{1,0:T(4,128)} %param.16) | copy-start | bytes 18436
  89.0 19.1 %copy-start.7 = (f32[512]{0:T(512)S(1)}, f32[512]{0:T(512)}, u32[]{:S(2)}) copy-start(f32[512]{0:T(512)} %param.18) | copy-start | bytes 6148
  89.0 19.3 %copy-start.9 = (s32[512]{0:T(512)S(1)}, s32[512]{0:T(512)}, u32[]{:S(2)}) copy-start(s32[512]{0:T(512)} %param.19) | copy-start | bytes 6148
  89.0 20.3 %copy-start.8 = (s32[1,128,1]{1,2,0:T(1,128)S(1)}, s32[1,128,1]{1,2,0:T(1,128)}, u32[]{:S(2)}) copy-start(s32[1,128,1]{1,2,0:T(1,128)} %param.20) | copy-start | bytes 1540
  102.0 9.3 %all-to-all-start.1 = ((f32[4,1,384]{2,1,0:T(1,128)}), f32[4,1,384]{2,1,0:T(1,128)S(1)}, u32[]{:S(2)}, u32[]{:S(2)}) async-start(f32[4,1,384]{2,1,0:T(1,128)} %reshape.253), calls=%async_computation.1 | async-start | bytes 12288 | tf_op jit(solution)/shard_map/all_to_all | solution.py:46
  111.3 24.0 %all-to-all-start = ((f32[128,1,128]{2,1,0:T(1,128)}), f32[128,1,128]{2,1,0:T(1,128)S(1)}, u32[]{:S(2)}, u32[]{:S(2)}) async-start(f32[128,1,128]{2,1,0:T(1,128)} %reshape.251), calls=%async_computation | async-start | bytes 131072 | tf_op jit(solution)/shard_map/all_to_all | solution.py:142
  146.3 6.1 %copy-start.3 = (f32[3,64]{1,0:T(4,128)S(1)}, f32[3,64]{1,0:T(4,128)}, u32[]{:S(2)}) copy-start(f32[3,64]{1,0:T(4,128)} %param.15) | copy-start | bytes 2308
  146.3 6.1 %copy-start.4 = (f32[3,64]{1,0:T(4,128)S(1)}, f32[3,64]{1,0:T(4,128)}, u32[]{:S(2)}) copy-start(f32[3,64]{1,0:T(4,128)} %param.14) | copy-start | bytes 2308
  146.3 6.1 %copy-start.5 = (f32[3,64]{1,0:T(4,128)S(1)}, f32[3,64]{1,0:T(4,128)}, u32[]{:S(2)}) copy-start(f32[3,64]{1,0:T(4,128)} %param.11) | copy-start | bytes 2308
  146.3 6.1 %copy-start.6 = (f32[3,64]{1,0:T(4,128)S(1)}, f32[3,64]{1,0:T(4,128)}, u32[]{:S(2)}) copy-start(f32[3,64]{1,0:T(4,128)} %param.12) | copy-start | bytes 2308
  146.3 6.7 %copy-start.1 = (f32[3,512]{1,0:T(4,128)S(1)}, f32[3,512]{1,0:T(4,128)}, u32[]{:S(2)}) copy-start(f32[3,512]{1,0:T(4,128)} %param.17) | copy-start | bytes 18436
where the time goes:
time: 154 us
  blocking collectives  61.4 us (40%)
  other arithmetic  58.4 us (38%)
  starting transfers between devices  15.4 us (10%)
  waiting for transfers between devices  11.4 us (7%)
  local copies, waits for them, and re-layouts  5.51 us (4%)
    all_gather x3, blocking collectives, stacked_from(): parts = lax.all_gather(parts, axes[k], axis=0, tiled=True)  43 us
    reduce_sum x5, other arithmetic, kernel(): dist_sq = jnp.sum(offset * offset, axis=0) + soften_sq  21.6 us
    all_gather x1, blocking collectives, body(): sibling = lax.all_gather(own_state, 'narrow', axis=1, tiled=True)  18.4 us
    reduce_sum x1, other arithmetic, kernel(): accel_sum = jnp.sum(offset * weight[None], axis=2)  12.2 us
    all_to_all x1, starting transfers between devices, body(): lax.all_to_all(outgoing, WIDE, split_axis=0, concat_axis=0, tiled=True)  10.7 us
    all_to_all x1, waiting for transfers between devices, body(): lax.all_to_all(outgoing, WIDE, split_axis=0, concat_axis=0, tiled=True)  10.6 us
    reduce_sum x4, other arithmetic, kernel(): return jnp.sum(offset * weight[None], axis=2)  7.87 us
    div x1, other arithmetic, kernel(): approach = 3.0 * jnp.sum(offset * rel_vel, axis=0) / dist_sq  6.96 us
  transfers between devices with their start and end apart: 2, of which 2 were waited for; matrix products, arithmetic and copies ran while one was open for 4% of the time, Pallas kernels for 0%

commit v1 on v0

v1 whole, which is shorter than its diff:
```python
import functools

import jax
import jax.numpy as jnp
from jax import lax
from jax.experimental import pallas as pl
from jax.experimental.pallas import tpu as pltpu
from jax.sharding import Mesh
from jax.sharding import PartitionSpec as P

GROUPS = 32
LEAF = 128
LANES = 128
TIME_STEP = 0.25
SOFT_SQ = 0.05
STEP_SQ = TIME_STEP * TIME_STEP
HIGHEST = lax.Precision.HIGHEST
F32 = jnp.float32

Z, XY, NARROW = "wide_z", "wide_xy", "narrow"
ALL = (Z, XY, NARROW)
N_Z, N_XY, N_NARROW = 16, 8, 4
STARS = 64
STAR_ROWS = 4


def predict(pos, vel, acc, jerk):
    pred_pos = pos + TIME_STEP * vel + STEP_SQ * 0.5 * acc + STEP_SQ * TIME_STEP / 6.0 * jerk
    pred_vel = vel + TIME_STEP * acc + STEP_SQ * 0.5 * jerk
    return pred_pos, pred_vel


def prepare_kernel(pos, vel, acc, jerk, mass, gpos, gmass, group, let, star_out, cells_out, send_out):
    pred_pos, pred_vel = predict(pos[...], vel[...], acc[...], jerk[...])
    zero = jnp.zeros((1, STARS), F32)
    rows = [
        (pred_pos[0:1], pred_pos[1:2]),
        (pred_pos[2:3], pred_vel[0:1]),
        (pred_vel[1:2], pred_vel[2:3]),
        (mass[...], zero),
    ]
    packed = jnp.concatenate([jnp.concatenate(pair, axis=1) for pair in rows], axis=0)
    packed = jnp.concatenate([packed, jnp.zeros((4, LANES), F32)], axis=0)
    for n in range(N_NARROW):
        star_out[n] = packed
    leaf_rows = []
    for leaf in range(4):
        span = pl.ds(leaf * LEAF, LEAF)
        m = gmass[:, span]
        stacked = jnp.concatenate([gpos[:, span] * m, m, jnp.zeros((4, LEAF), F32)], axis=0)
        onehot = jnp.where(
            lax.broadcasted_iota(jnp.int32, (GROUPS, LEAF), 0) == group[:, span], 1.0, 0.0
        )
        sums = lax.dot_general(
            stacked, onehot, (((1,), (1,)), ((), ())), precision=HIGHEST, preferred_element_type=F32
        )
        total = sums[3:4]
        centre = sums[0:3] / total
        leaf_rows.append(
            jnp.concatenate([centre[0:1], centre[1:2], centre[2:3], total], axis=1)
        )
    cells_out[...] = jnp.concatenate(leaf_rows + [jnp.zeros((4, LANES), F32)], axis=0)
    ids = jnp.broadcast_to(let[...], (N_Z * N_XY, LANES))
    chosen = jnp.zeros((N_Z * N_XY, LANES), F32)
    for leaf in range(4):
        chosen = jnp.where(ids == leaf, jnp.broadcast_to(leaf_rows[leaf], chosen.shape), chosen)
    for z in range(N_Z):
        send_out[z, 0:8] = chosen[8 * z : 8 * z + 8]
        send_out[z, 8:16] = packed


def low_lanes(shape):
    return lax.broadcasted_iota(jnp.int32, shape, 1) < 64


def star_planes(stars, planes, count):
    half = N_XY // 2 * N_Z
    low = low_lanes((half, LANES))
    for r in range((count + 1) // 2):
        picked = [stars[e, pl.ds(r, N_Z, stride=STAR_ROWS), :] for e in range(N_XY)]
        first = jnp.concatenate(picked[: N_XY // 2], axis=0)
        second = jnp.concatenate(picked[N_XY // 2 :], axis=0)
        planes[2 * r] = jnp.where(low, first, pltpu.roll(second, 64, 1))
        if 2 * r + 1 < count:
            planes[2 * r + 1] = jnp.where(low, pltpu.roll(first, 64, 1), second)


def row_sums(x):
    return lax.dot_general(
        jnp.ones((8, LANES), F32), x, (((1,), (1,)), ((), ())), precision=HIGHEST, preferred_element_type=F32
    )


def hermite_kernel(sib, stars, out, planes, tgt, sums):
    star_planes(stars, planes, 7)
    for n in range(N_NARROW):
        turned = jnp.transpose(sib[n])
        for c in range(6):
            col = turned[64 * (c % 2) : 64 * (c % 2) + 64, c // 2 : c // 2 + 1]
            tgt[c, n * STARS : (n + 1) * STARS] = jnp.broadcast_to(col, (STARS, LANES))
    chunk = 16
    n_rows = planes.shape[1]

    @pl.loop(0, N_NARROW * STARS // chunk)
    def _(i):
        at = pl.ds(pl.multiple_of(i * chunk, chunk), chunk)
        px, py, pz, vx, vy, vz = [tgt[c, at, :] for c in range(6)]

        def step(r, carry):
            ax, ay, az, jx, jy, jz = carry
            qx, qy, qz, ux, uy, uz, m = [
                jnp.broadcast_to(planes[c, pl.ds(r, 1), :], (chunk, LANES)) for c in range(7)
            ]
            dx, dy, dz = qx - px, qy - py, qz - pz
            du, dv, dw = ux - vx, uy - vy, uz - vz
            dist = dx * dx + dy * dy + dz * dz + SOFT_SQ
            inv = lax.rsqrt(dist)
            inv2 = inv * inv
            w = m * inv * inv2
            far = (dx * du + dy * dv + dz * dw) * inv2 * 3.0
            wf = w * far
            return (
                ax + w * dx,
                ay + w * dy,
                az + w * dz,
                jx + (w * du - wf * dx),
                jy + (w * dv - wf * dy),
                jz + (w * dw - wf * dz),
            )

        zero = jnp.zeros((chunk, LANES), F32)
        res = lax.fori_loop(0, n_rows, step, (zero,) * 6, unroll=4)
        for c in range(6):
            sums[c, at, :] = res[c]

    for c in range(6):
        row = row_sums(sums[c])[0:1]
        for n in range(N_NARROW):
            out[n, c : c + 1, 0:STARS] = row[:, n * STARS : (n + 1) * STARS]


def pull_kernel(
    leaf_ref, gpos, gvel, gmass, stars, own, cells, gal_out, cell_out, planes, splanes, cplanes, tgt, stgt, sums
):
    quarter = N_XY // 4
    lane_group = lax.broadcasted_iota(jnp.int32, (32, LANES), 1) // GROUPS
    parts = [
        jnp.concatenate([stars[e, 64:80, :] for e in range(quarter * k, quarter * (k + 1))], axis=0)
        for k in range(4)
    ]
    for c in range(4):
        plane = parts[c]
        for k in range(4):
            if k != c:
                plane = jnp.where(lane_group == k, pltpu.roll(parts[k], (GROUPS * (k - c)) % LANES, 1), plane)
        planes[c, 0:32] = plane
    one_group = lax.broadcasted_iota(jnp.int32, (1, LANES), 1) // GROUPS
    for c in range(4):
        row = cells[c : c + 1]
        for k in range(4):
            if k != c:
                row = jnp.where(one_group == k, pltpu.roll(cells[k : k + 1], (GROUPS * (k - c)) % LANES, 1), row)
        cplanes[c : c + 1] = row
    for leaf in range(4):
        span = pl.ds(leaf * LEAF, LEAF)
        for c in range(3):
            planes[c, 32 + leaf : 33 + leaf] = gpos[c : c + 1, span]
        planes[3, 32 + leaf : 33 + leaf] = gmass[:, span]
    star_planes(stars, splanes, 7)
    low = low_lanes((1, LANES))
    for leaf in range(4):
        for pair in range(4):
            picks = []
            for side in range(2):
                b = leaf_ref[leaf, 2 * pair + side]
                place = (b % N_XY) * N_Z + b // N_XY
                upper = place // 64
                picks.append((place - 64 * upper, upper))
            for c in range(4):
                plane = c if c < 3 else 6
                sides = []
                for side in range(2):
                    at, upper = picks[side]
                    row = splanes[plane, pl.ds(at, 1), :]
                    sides.append(jnp.where(upper == side, row, pltpu.roll(row, 64, 1)))
                planes[c, 36 + 4 * leaf + pair : 37 + 4 * leaf + pair] = jnp.where(low, sides[0], sides[1])
    for leaf in range(4):
        span = pl.ds(leaf * LEAF, LEAF)
        block = jnp.concatenate([gpos[:, span], jnp.zeros((5, LEAF), F32)], axis=0)
        turned = jnp.transpose(block)
        for c in range(3):
            tgt[c, leaf * LEAF : (leaf + 1) * LEAF] = jnp.broadcast_to(turned[:, c : c + 1], (LEAF, LANES))
    turned = jnp.transpose(own[...])
    for c in range(3):
        stgt[c] = jnp.broadcast_to(
            turned[64 * (c % 2) : 64 * (c % 2) + 64, c // 2 : c // 2 + 1], (STARS, LANES)
        )
    chunk = 32

    def add_pull(source, here, total):
        dx, dy, dz = [jnp.broadcast_to(source[c], here[c].shape) - here[c] for c in range(3)]
        inv = lax.rsqrt(dx * dx + dy * dy + dz * dz + SOFT_SQ)
        w = jnp.broadcast_to(source[3], here[0].shape) * inv * (inv * inv)
        return total[0] + w * dx, total[1] + w * dy, total[2] + w * dz

    def source_at(r):
        return [planes[c, pl.ds(r, 1), :] for c in range(4)]

    zero = jnp.zeros((chunk, LANES), F32)

    @pl.loop(0, 4 * LEAF // chunk)
    def _(i):
        at = pl.ds(pl.multiple_of(i * chunk, chunk), chunk)
        here = [tgt[c, at, :] for c in range(3)]
        res = lax.fori_loop(0, 36, lambda r, t: add_pull(source_at(r), here, t), (zero,) * 3, unroll=4)
        first = 36 + 4 * (i // (LEAF // chunk))
        for k in range(4):
            res = add_pull(source_at(first + k), here, res)
        for c in range(3):
            sums[c, at, :] = res[c]

    for c in range(3):
        gal_out[c : c + 1] = gvel[c : c + 1] + TIME_STEP * row_sums(sums[c])[0:1]

    for i in range(STARS // chunk):
        here = [stgt[c, i * chunk : (i + 1) * chunk, :] for c in range(3)]
        res = lax.fori_loop(0, 32, lambda r, t: add_pull(source_at(r), here, t), (zero,) * 3, unroll=4)
        res = add_pull([cplanes[c : c + 1] for c in range(4)], here, res)
        for c in range(3):
            sums[c, i * chunk : (i + 1) * chunk, :] = res[c]
    for c in range(3):
        cell_out[c : c + 1, 0:STARS] = row_sums(sums[c, 0:STARS])[0:1]


def correct_kernel(pos, vel, acc, jerk, parts, cell, pos_out, vel_out):
    summed = parts[0] + parts[1] + parts[2] + parts[3]
    new_acc = summed[0:3, 0:STARS] + cell[0:3, 0:STARS]
    new_jerk = summed[3:6, 0:STARS]
    new_vel = (
        vel[...]
        + TIME_STEP * 0.5 * (acc[...] + new_acc)
        + STEP_SQ / 12.0 * (jerk[...] - new_jerk)
    )
    vel_out[...] = new_vel
    pos_out[...] = (
        pos[...]
        + TIME_STEP * 0.5 * (vel[...] + new_vel)
        + STEP_SQ / 12.0 * (acc[...] - new_acc)
    )


def shape(*lengths):
    return jax.ShapeDtypeStruct(lengths, F32)


VMEM_SPEC = pl.BlockSpec(memory_space=pltpu.VMEM)
PARAMS = pltpu.CompilerParams(vmem_limit_bytes=32 * 1024 * 1024)


def body(
    star_pos, star_vel, star_mass, star_acc, star_jerk, gal_pos, gal_vel, gal_mass, group_of, let_send, star_leaf
):
    star_rows, cells, send = pl.pallas_call(
        prepare_kernel,
        out_shape=(shape(N_NARROW, 8, LANES), shape(8, LANES), shape(N_Z, 16, LANES)),
        in_specs=[VMEM_SPEC] * 9,
        out_specs=(VMEM_SPEC,) * 3,
        compiler_params=PARAMS,
    )(
        star_pos,
        star_vel,
        star_acc,
        star_jerk,
        star_mass.reshape(1, -1),
        gal_pos,
        gal_mass.reshape(1, -1),
        group_of.reshape(1, -1),
        let_send.reshape(-1, 1),
    )
    arrived = lax.all_to_all(send, Z, split_axis=0, concat_axis=0, tiled=True)
    siblings = lax.all_to_all(star_rows, NARROW, split_axis=0, concat_axis=0, tiled=True)
    star_part = arrived[:, 8:12].reshape(1, N_Z * STAR_ROWS, LANES)
    cell_part = arrived[:, 0:8].transpose(1, 0, 2)
    onward = jnp.concatenate(
        [jnp.broadcast_to(star_part, (N_XY, *star_part.shape[1:])), cell_part], axis=1
    )
    stars = lax.all_to_all(onward, XY, split_axis=0, concat_axis=0, tiled=True)
    partial = pl.pallas_call(
        hermite_kernel,
        out_shape=shape(N_NARROW, 8, LANES),
        in_specs=[VMEM_SPEC] * 2,
        out_specs=VMEM_SPEC,
        scratch_shapes=[
            pltpu.VMEM((7, 64, LANES), F32),
            pltpu.VMEM((6, N_NARROW * STARS, LANES), F32),
            pltpu.VMEM((6, N_NARROW * STARS, LANES), F32),
        ],
        compiler_params=PARAMS,
        cost_estimate=pl.CostEstimate(flops=80_000_000, bytes_accessed=400_000, transcendentals=2_000_000),
    )(siblings, stars)
    shared = lax.all_to_all(partial, NARROW, split_axis=0, concat_axis=0, tiled=True)
    gal_vel_new, cell_acc = pl.pallas_call(
        pull_kernel,
        out_shape=(shape(3, 4 * LEAF), shape(8, LANES)),
        in_specs=[pl.BlockSpec(memory_space=pltpu.SMEM)] + [VMEM_SPEC] * 6,
        out_specs=(VMEM_SPEC,) * 2,
        scratch_shapes=[
            pltpu.VMEM((4, 56, LANES), F32),
            pltpu.VMEM((7, 64, LANES), F32),
            pltpu.VMEM((8, LANES), F32),
            pltpu.VMEM((3, 4 * LEAF, LANES), F32),
            pltpu.VMEM((3, STARS, LANES), F32),
            pltpu.VMEM((3, 4 * LEAF, LANES), F32),
        ],
        compiler_params=PARAMS,
        cost_estimate=pl.CostEstimate(flops=60_000_000, bytes_accessed=400_000, transcendentals=3_000_000),
    )(star_leaf, gal_pos, gal_vel, gal_mass.reshape(1, -1), stars, star_rows[0], cells)
    star_pos_new, star_vel_new = pl.pallas_call(
        correct_kernel,
        out_shape=(shape(3, STARS), shape(3, STARS)),
        in_specs=[VMEM_SPEC] * 6,
        out_specs=(VMEM_SPEC,) * 2,
        compiler_params=PARAMS,
    )(star_pos, star_vel, star_acc, star_jerk, shared, cell_acc)
    return gal_vel_new, star_pos_new, star_vel_new


def solution(mesh):
    torus = Mesh(mesh.devices.reshape(N_Z, N_XY, N_NARROW), ALL)
    cols = P(None, ALL)
    return jax.shard_map(
        body,
        mesh=torus,
        in_specs=(
            cols,
            cols,
            P(ALL),
            cols,
            cols,
            cols,
            cols,
            P(ALL),
            P(ALL),
            P(ALL, None, None),
            P(ALL, None),
        ),
        out_specs=(cols, cols, cols),
        check_vma=False,
    )
```

time: 154 us -> 87.1 us (0.57)
  other arithmetic: 58.4 us -> 0.02 us
  Pallas kernels: 0 us -> 27.5 us
  blocking collectives: 61.4 us -> 38 us
  waiting for transfers between devices: 11.4 us -> 4.54 us
  local copies, waits for them, and re-layouts: 5.51 us -> 2.2 us
  starting transfers between devices: 15.4 us -> 13.7 us
    all_gather x4 -> x0, blocking collectives: 61.4 us -> none  [the longest x3 43 us: stacked_from(): parts = lax.all_gather(parts, axes[k], axis=0, tiled=True)]
    reduce_sum x11 -> x0, other arithmetic: 41.7 us -> none  [the longest x5 21.6 us: kernel(): dist_sq = jnp.sum(offset * offset, axis=0) + soften_sq]
    all_to_all x0 -> x2, blocking collectives: none -> 38 us  [the longest x1 27.5 us: body(): arrived = lax.all_to_all(send, Z, split_axis=0, concat_axis=0, tiled=True)]
    pallas_call x0 -> x4, Pallas kernels: none -> 27.5 us  [the longest x1 14.9 us: body(): pl.pallas_call(hermite_kernel, out_shape=shape(N_NARROW, 8, LANES), in_sp...]
    div x1 -> x0, other arithmetic: 6.96 us -> none  [kernel(): approach = 3.0 * jnp.sum(offset * rel_vel, axis=0) / dist_sq]
    all_to_all x2, waiting for transfers between devices: 11.4 us -> 4.54 us  [the longest x1 4.54 us: body(): lax.all_to_all(star_rows, NARROW, split_axis=0, concat_axis=0, tiled=True)]
    mul x4 -> x0, other arithmetic: 5.51 us -> none  [kernel(): weight = src_mass[None, :] * inverse * inverse * inverse]
    add x3 -> x0, other arithmetic: 1.94 us -> none  [the longest x1 0.74 us: body(): star_pos + time_step * star_vel + step_sq * 0.5 * star_acc]
  transfers between devices with their start and end apart: 2 -> 2, of which waited for: 2 -> 1; matrix products, arithmetic and copies ran while one was open for 4% -> 1% of each run, Pallas kernels for 0% -> 13%
where the time goes in v1:
time: 87.1 us; the launch traced here: 86.7 us
  blocking collectives  38 us (44%)
  Pallas kernels  27.5 us (32%)
  starting transfers between devices  13.7 us (16%)
  waiting for transfers between devices  4.54 us (5%)
  local copies, waits for them, and re-layouts  2.2 us (3%)
    all_to_all x1, blocking collectives, body(): arrived = lax.all_to_all(send, Z, split_axis=0, concat_axis=0, tiled=True)  27.5 us
    pallas_call x1, Pallas kernels, body(): pl.pallas_call(hermite_kernel, out_shape=shape(N_NARROW, 8, LANES), in_sp...  14.9 us
    pallas_call x1, Pallas kernels, body(): pl.pallas_call(pull_kernel, out_shape=(shape(3, 4 * LEAF), shape(8, LANES...  11.3 us
    all_to_all x1, blocking collectives, body(): stars = lax.all_to_all(onward, XY, split_axis=0, concat_axis=0, tiled=True)  10.5 us
    all_to_all x1, starting transfers between devices, body(): lax.all_to_all(star_rows, NARROW, split_axis=0, concat_axis=0, tiled=True)  8.12 us
    all_to_all x1, starting transfers between devices, body(): lax.all_to_all(partial, NARROW, split_axis=0, concat_axis=0, tiled=True)  5.62 us
    all_to_all x1, waiting for transfers between devices, body(): lax.all_to_all(star_rows, NARROW, split_axis=0, concat_axis=0, tiled=True)  4.54 us
  transfers between devices with their start and end apart: 2, of which 1 were waited for; matrix products, arithmetic and copies ran while one was open for 1% of the time, Pallas kernels for 13%

profile of v1, /device:TPU:1, one launch (start us, length us, event | category | flops | bytes accessed | tf_op | source)
XLA Modules:
  0.0 86.7 jit_solution(8918870767405899073)
XLA Ops:
  0.6 0.0 copy-start.10
  0.6 0.6 copy-done.10
  1.3 0.0 copy-start.6
  1.3 0.1 copy.19.let
  1.4 0.0 copy-start
  1.4 0.0 copy-start.7
  1.5 0.5 copy-done.2
  2.0 0.0 copy-done.3
  2.0 0.0 copy-done.4
  2.0 0.0 copy-done.5
  2.0 0.0 copy-done.6
  2.0 0.1 copy-done.1
  2.1 0.0 copy-done
  2.1 0.7 shard_map.130
  2.8 27.5 %all_to_all.20 = f32[16,16,128]{2,1,0:T(8,128)S(1)} all-to-all(f32[16,16,128]{2,1,0:T(8,128)S(1)} %get-tuple-element.10), channel_id=1, replica_groups=mesh['wide_z'=16,'wide_xy'=8,'narrow'=4] {'wide_z'}, dimensions={0} | all-to-all | bytes 262144 | tf_op jit(solution)/shard_map/all_to_all | solution.py:280
  30.4 8.1 %all-to-all-start.2 = ((f32[4,8,128]{2,1,0:T(8,128)}), f32[4,8,128]{2,1,0:T(8,128)S(1)}, u32[]{:S(2)}, u32[]{:S(2)}) async-start(f32[4,8,128]{2,1,0:T(8,128)} %get-tuple-element.11), calls=%async_computation.2 | async-start | bytes 32768 | tf_op jit(solution)/shard_map/all_to_all | solution.py:281
  38.6 4.5 %all-to-all-done.2.sib = f32[4,8,128]{2,1,0:T(8,128)S(1)} async-done(((f32[4,8,128]{2,1,0:T(8,128)}), f32[4,8,128]{2,1,0:T(8,128)S(1)}, u32[]{:S(2)}, u32[]{:S(2)}) %all-to-all-start.2) | async-done | bytes 16416 | tf_op jit(solution)/shard_map/all_to_all | solution.py:281
  43.1 10.5 %all_to_all.21.stars = f32[8,80,128]{2,1,0:T(8,128)S(1)} all-to-all(f32[8,80,128]{2,1,0:T(8,128)S(1)} %pad_maximum_fusion), channel_id=1, replica_groups=mesh['wide_z'=16,'wide_xy'=8,'narrow'=4] {'wide_xy'}, dimensions={0} | all-to-all | bytes 655360 | tf_op jit(solution)/shard_map/all_to_all | solution.py:287
  53.6 14.9 %shard_map.132 = f32[4,8,128]{2,1,0:T(8,128)} custom-call(f32[4,8,128]{2,1,0:T(8,128)S(1)} %all-to-all-done.2.sib, f32[8,80,128]{2,1,0:T(8,128)S(1)} %all_to_all.21.stars), custom_call_target="tpu_custom_call" | custom-call | flops 80000000 | bytes 400000 | tf_op jit(solution)/shard_map/pallas_call | solution.py:288
  68.5 5.6 %all-to-all-start.3 = ((f32[4,8,128]{2,1,0:T(8,128)}), f32[4,8,128]{2,1,0:T(8,128)S(1)}, u32[]{:S(2)}, u32[]{:S(2)}) async-start(f32[4,8,128]{2,1,0:T(8,128)} %shard_map.132), calls=%async_computation.3 | async-start | bytes 32768 | tf_op jit(solution)/shard_map/all_to_all | solution.py:301
  74.1 0.7 slice_bitcast_fusion.own
  74.8 11.3 %shard_map.131 = (f32[3,512]{1,0:T(4,128)}, f32[8,128]{1,0:T(8,128)S(1)}) custom-call(s32[4,8]{1,0:T(4,128)S(1)} %copy-done.9, f32[3,512]{1,0:T(4,128)S(1)} %copy-done.4, f32[3,512]{1,0:T(4,128)S(1)} %copy-done.8, f32[1,512]{1,0:T(1,128)S(1)} %bitcast.12, f32[8,80,128]{2,1,0:T(8,128)S(1)} %all_to_all.21.stars, f32[8,128]{1,0:T(8,128)S(1)} %slice_bitcast_fusion.own, ...), custom_call_target="tpu_custom_call" | custom-call | flops 60000000 | bytes 400000 | tf_op jit(solution)/shard_map/pallas_call | solution.py:302
  86.1 0.0 all-to-all-done.3.parts
  86.1 0.6 shard_map.133
  (15 shorter events, 0.1 us)
Async XLA Ops:
  0.6 0.7 copy-start.10
  1.3 0.7 copy-start.2
  1.3 0.7 copy-start.3
  1.3 0.7 copy-start.4
  1.3 0.7 copy-start.5
  1.3 0.7 copy-start.6
  1.4 0.7 copy-start.1
  1.4 0.7 copy-start
  1.4 0.7 copy-start.7
  30.4 12.7 %all-to-all-start.2 = ((f32[4,8,128]{2,1,0:T(8,128)}), f32[4,8,128]{2,1,0:T(8,128)S(1)}, u32[]{:S(2)}, u32[]{:S(2)}) async-start(f32[4,8,128]{2,1,0:T(8,128)} %get-tuple-element.11), calls=%async_computation.2 | async-start | bytes 32768 | tf_op jit(solution)/shard_map/all_to_all | solution.py:281
  53.6 21.2 %copy-start.9 = (s32[4,8]{1,0:T(4,128)S(1)}, s32[4,8]{1,0:T(4,128)}, u32[]{:S(2)}) copy-start(s32[4,8]{1,0:T(4,128)} %leaf_ref.1) | copy-start | bytes 388
  68.5 17.6 %all-to-all-start.3 = ((f32[4,8,128]{2,1,0:T(8,128)}), f32[4,8,128]{2,1,0:T(8,128)S(1)}, u32[]{:S(2)}, u32[]{:S(2)}) async-start(f32[4,8,128]{2,1,0:T(8,128)} %shard_map.132), calls=%async_computation.3 | async-start | bytes 32768 | tf_op jit(solution)/shard_map/all_to_all | solution.py:301
  74.1 0.7 copy-start.8

commit v2 on v1

v2 whole, which is shorter than its diff:
```python
import jax
import jax.numpy as jnp
from jax import lax
from jax.experimental import pallas as pl
from jax.experimental.pallas import tpu as pltpu
from jax.sharding import Mesh
from jax.sharding import PartitionSpec as P

GROUPS = 32
LEAF = 128
LANES = 128
TIME_STEP = 0.25
SOFT_SQ = 0.05
STEP_SQ = TIME_STEP * TIME_STEP
HIGHEST = lax.Precision.HIGHEST
F32, BF16 = jnp.float32, jnp.bfloat16
LANE_BY_LANE = (((1,), (1,)), ((), ()))

Z, XY, NARROW = "wide_z", "wide_xy", "narrow"
ALL = (Z, XY, NARROW)
N_Z, N_XY, N_NARROW = 16, 8, 4
STARS = 64
STAR_ROWS = 4
PER_BLOCK = 2 * LANES


def predict(pos, vel, acc, jerk):
    pred_pos = pos + TIME_STEP * vel + STEP_SQ * 0.5 * acc + STEP_SQ * TIME_STEP / 6.0 * jerk
    pred_vel = vel + TIME_STEP * acc + STEP_SQ * 0.5 * jerk
    return pred_pos, pred_vel


def prepare_kernel(pos, vel, acc, jerk, mass, gpos, gmass, group, let, star_out, own_out, cells_out, send_out):
    pred_pos, pred_vel = predict(pos[...], vel[...], acc[...], jerk[...])
    zero = jnp.zeros((1, STARS), F32)
    rows = [
        (pred_pos[0:1], pred_pos[1:2]),
        (pred_pos[2:3], pred_vel[0:1]),
        (pred_vel[1:2], pred_vel[2:3]),
        (mass[...], zero),
    ]
    packed = jnp.concatenate([jnp.concatenate(pair, axis=1) for pair in rows], axis=0)
    own = jnp.concatenate([packed, jnp.zeros((4, LANES), F32)], axis=0)
    own_out[...] = own
    for n in range(N_NARROW):
        star_out[n] = own
    leaf_rows = []
    for leaf in range(4):
        span = pl.ds(leaf * LEAF, LEAF)
        m = gmass[:, span]
        stacked = jnp.concatenate([gpos[:, span] * m, m, jnp.zeros((4, LEAF), F32)], axis=0)
        onehot = jnp.where(
            lax.broadcasted_iota(jnp.int32, (GROUPS, LEAF), 0) == group[:, span], 1.0, 0.0
        )
        sums = lax.dot_general(stacked, onehot, LANE_BY_LANE, precision=HIGHEST, preferred_element_type=F32)
        total = sums[3:4]
        centre = sums[0:3] / total
        leaf_rows.append(
            jnp.concatenate([centre[0:1], centre[1:2], centre[2:3], total], axis=1)
        )
    cells_out[...] = jnp.concatenate(leaf_rows + [jnp.zeros((4, LANES), F32)], axis=0)
    ids = let[...].astype(F32)
    lane = lax.broadcasted_iota(jnp.int32, (1, LANES), 1)
    listed = jnp.logical_and(lane >= 64, lane < 64 + N_XY)
    for z in range(N_Z):
        turned = pltpu.roll(ids, (64 - N_XY * z) % LANES, 1)
        last = jnp.where(listed, turned, packed[3:4])
        send_out[z] = jnp.concatenate([packed[0:3], last] + leaf_rows, axis=0)


def onward_kernel(arrived, out):
    flat = arrived
    for pair in range(N_Z // 2):
        both = jnp.concatenate(
            [flat[16 * pair : 16 * pair + 4, :], flat[16 * pair + 8 : 16 * pair + 12, :]], axis=0
        )
        for e in range(N_XY):
            out[e, 8 * pair : 8 * pair + 8, :] = both
    ids = flat[pl.ds(3, N_Z, stride=8), :]
    cells = [flat[pl.ds(4 + leaf, N_Z, stride=8), :] for leaf in range(4)]
    for e in range(N_XY):
        which = jnp.broadcast_to(ids[:, 64 + e : 65 + e], (N_Z, LANES))
        rows = jnp.zeros((N_Z, LANES), F32)
        for leaf in range(4):
            rows = jnp.where(which == float(leaf), cells[leaf], rows)
        out[e, 64:80, :] = rows


def low_lanes(shape):
    return lax.broadcasted_iota(jnp.int32, shape, 1) < 64


def star_plane_pair(stars, r):
    low = low_lanes((N_XY // 2 * N_Z, LANES))
    picked = [stars[e, pl.ds(r, N_Z, stride=STAR_ROWS), :] for e in range(N_XY)]
    first = jnp.concatenate(picked[: N_XY // 2], axis=0)
    second = jnp.concatenate(picked[N_XY // 2 :], axis=0)
    return (
        jnp.where(low, first, pltpu.roll(second, 64, 1)),
        jnp.where(low, pltpu.roll(first, 64, 1), second),
    )


def row_sums(x):
    ones = jnp.ones((8, LANES), F32)
    return lax.dot_general(ones, x, LANE_BY_LANE, precision=HIGHEST, preferred_element_type=F32)[0:1]


def split3(x):
    high = x.astype(BF16).astype(F32)
    rest = x - high
    middle = rest.astype(BF16).astype(F32)
    return high, middle, rest - middle


def source_slots(x):
    h, m, l = split3(x)
    none = jnp.zeros_like(x)
    return jnp.concatenate([h, h, h, m, m, l, none, none], axis=0).astype(BF16)


def target_slots(x):
    h, m, l = split3(x)
    rows = jnp.concatenate([h, m, l, h, m, h] + [jnp.zeros_like(x)] * 10, axis=0)
    return jnp.transpose(rows)[:, 0:64].astype(BF16)


def weighted(source, weight):
    h, m, l = split3(source)
    parts = jnp.concatenate([h, m, l, jnp.zeros_like(source)], axis=0).astype(BF16)
    high = weight.astype(BF16)
    low = (weight - high.astype(F32)).astype(BF16)
    return lax.dot_general(parts, high, LANE_BY_LANE, preferred_element_type=F32) + lax.dot_general(
        parts, low, LANE_BY_LANE, preferred_element_type=F32
    )


def add_parts(x):
    return x[0:8] + x[8:16] + x[16:24]


def twice(x):
    return jnp.concatenate([x, x], axis=1)


def store_rows(ref, stride, row, plane):
    blocks = plane.shape[0] // 2
    ref[0, pl.ds(row, blocks, stride=stride), :] = plane[:blocks]
    ref[1, pl.ds(row, blocks, stride=stride), :] = plane[blocks:]


def load_block(ref, at):
    return jnp.concatenate([ref[half, pl.ds(at, 8), :] for half in range(2)], axis=1)


def hermite_kernel(sib, stars, out, table, slots, here, main, drag):
    n_targets = N_NARROW * STARS
    x, y = star_plane_pair(stars, 0)
    z, u = star_plane_pair(stars, 1)
    v, w = star_plane_pair(stars, 2)
    m, _ = star_plane_pair(stars, 3)
    product = m * (x * u + y * v + z * w)
    for row, plane in enumerate((x, y, z)):
        store_rows(table, 16, row, plane)
    for row, plane in enumerate((m * x, m * y, m * z, m * u, m * v, m * w, m, product)):
        store_rows(table, 16, 8 + row, plane)
    comps = [[] for _ in range(6)]
    for n in range(N_NARROW):
        block = sib[n]
        for c in range(6):
            comps[c].append(block[c // 2 : c // 2 + 1, 64 * (c % 2) : 64 * (c % 2) + 64])
    rows = [jnp.concatenate(parts, axis=1) for parts in comps]
    p = jnp.concatenate(rows[0:3], axis=0)
    q = jnp.concatenate(rows[3:6], axis=0)
    own_product = jnp.sum(p * q, axis=0, keepdims=True)
    slots[...] = target_slots(
        jnp.concatenate([-q, -p, own_product, jnp.ones((1, n_targets), F32)], axis=0)
    )
    turned = jnp.transpose(jnp.concatenate([p, jnp.zeros((5, n_targets), F32)], axis=0))
    for c in range(3):
        here[c] = jnp.broadcast_to(turned[:, c : c + 1], (n_targets, LANES))
    main[...] = jnp.zeros(main.shape, F32)
    drag[...] = jnp.zeros(drag.shape, F32)

    def block(b, _):
        at = pl.multiple_of(b * 16, 16)
        g = load_block(table, at)
        s = load_block(table, at + 8)
        dx, dy, dz = [g[c : c + 1] - twice(here[c]) for c in range(3)]
        inv = lax.rsqrt(dx * dx + (dy * dy + (dz * dz + SOFT_SQ)))
        approach = jnp.dot(slots[...], source_slots(s), preferred_element_type=F32)
        inv2 = inv * inv
        weight = inv * inv2
        main[...] += weighted(s, weight)
        pulled = weight * inv2 * approach
        for c, d in enumerate((dx, dy, dz)):
            term = pulled * d
            drag[c] += term[:, 0:LANES] + term[:, LANES:PER_BLOCK]
        return 0

    lax.fori_loop(0, table.shape[1] // 16, block, 0, unroll=4)
    total = add_parts(main[...])
    accel = total[0:3] - p * total[6:7]
    dragged = jnp.concatenate([row_sums(drag[c]) for c in range(3)], axis=0)
    jerk = total[3:6] - q * total[6:7] - 3.0 * dragged
    both = jnp.concatenate([accel, jerk, jnp.zeros((2, n_targets), F32)], axis=0)
    for n in range(N_NARROW):
        out[n, :, 0:STARS] = both[:, n * STARS : (n + 1) * STARS]


CELL_BLOCKS = 16
BODY_BLOCK = 16
STAR_BLOCK = 18
BLOCKS = 26


def by_group(picked):
    lane_group = lax.broadcasted_iota(jnp.int32, picked[0].shape, 1) // GROUPS
    out = []
    for c in range(4):
        plane = picked[c]
        for k in range(4):
            if k != c:
                plane = jnp.where(lane_group == k, pltpu.roll(picked[k], (GROUPS * (k - c)) % LANES, 1), plane)
        out.append(plane)
    return out


def table_rows(x, y, z, m):
    return (x, y, z, m * x, m * y, m * z, m)


def build_table(leaf_ref, gpos, gmass, stars, table, splanes):
    quarter = N_XY // 4
    parts = [
        jnp.concatenate([stars[e, 64:80, :] for e in range(quarter * k, quarter * (k + 1))], axis=0)
        for k in range(4)
    ]
    for row, plane in enumerate(table_rows(*by_group(parts))):
        store_rows(table, 8, row, plane)
    for half in range(2):
        spot = slice(8 * (BODY_BLOCK + half), 8 * (BODY_BLOCK + half) + 7)
        for side in range(2):
            span = slice(half * PER_BLOCK + side * LANES, half * PER_BLOCK + (side + 1) * LANES)
            m = gmass[:, span]
            table[side, spot, :] = jnp.concatenate([gpos[:, span], gpos[:, span] * m, m], axis=0)
    x, y = star_plane_pair(stars, 0)
    z, _ = star_plane_pair(stars, 1)
    m, _ = star_plane_pair(stars, 3)
    for c, plane in enumerate((x, y, z, m)):
        splanes[pl.ds(c, 64, stride=8), :] = plane
    low = low_lanes((8, LANES))
    for leaf in range(4):
        for pair in range(4):
            sides = []
            for side in range(2):
                b = leaf_ref[leaf, 2 * pair + side]
                place = (b % N_XY) * N_Z + b // N_XY
                upper = place // 64
                rows = splanes[pl.ds(pl.multiple_of((place - 64 * upper) * 8, 8), 8), :]
                sides.append(jnp.where(upper == side, rows, pltpu.roll(rows, 64, 1)))
            rows = jnp.where(low, sides[0], sides[1])
            m = rows[3:4]
            first = 8 * (STAR_BLOCK + 2 * leaf + pair // 2)
            table[pair % 2, first : first + 7, :] = jnp.concatenate(
                [rows[0:3], rows[0:3] * m, m], axis=0
            )


def pull_of(block, here):
    dx, dy, dz = [block[c : c + 1] - here[c] for c in range(3)]
    inv = lax.rsqrt(dx * dx + (dy * dy + (dz * dz + SOFT_SQ)))
    return weighted(block, inv * (inv * inv))


def pull_leaves(first, gpos, gvel, table, here, total, gal_out):
    count = 2 * LEAF
    span = slice(first * LEAF, first * LEAF + count)
    p = gpos[:, span]
    turned = jnp.transpose(jnp.concatenate([p, jnp.zeros((5, count), F32)], axis=0))
    for c in range(3):
        here[c, 0:count] = jnp.broadcast_to(turned[:, c : c + 1], (count, LANES))
    total[...] = jnp.zeros(total.shape, F32)

    def block(b, _):
        g = load_block(table, pl.multiple_of(b * 8, 8))
        total[...] += pull_of(g, [twice(here[c, 0:count]) for c in range(3)])
        return 0

    lax.fori_loop(0, STAR_BLOCK, block, 0, unroll=3)
    for k in range(2):
        lanes = slice(k * LEAF, (k + 1) * LEAF)
        for half in range(2):
            at = 8 * (STAR_BLOCK + 2 * (first + k) + half)
            total[:, lanes] += pull_of(load_block(table, at), [twice(here[c, lanes]) for c in range(3)])
    summed = add_parts(total[...])
    gal_out[...] = gvel[:, span] + TIME_STEP * (summed[3:6] - p * summed[6:7])


def first_pull_kernel(leaf_ref, gpos, gvel, gmass, stars, gal_out, table, splanes, here, total):
    table[...] = jnp.zeros(table.shape, F32)
    splanes[...] = jnp.zeros(splanes.shape, F32)
    build_table(leaf_ref, gpos, gmass, stars, table, splanes)
    pull_leaves(0, gpos, gvel, table, here, total, gal_out)


def second_pull_kernel(gpos, gvel, own, cells, table, gal_out, cell_out, here, total, star_total):
    pull_leaves(2, gpos, gvel, table, here, total, gal_out)
    turned = jnp.transpose(own[...])
    for c in range(3):
        column = turned[64 * (c % 2) : 64 * (c % 2) + 64, c // 2 : c // 2 + 1]
        here[c, 0:STARS] = jnp.broadcast_to(column, (STARS, LANES))
    star_total[...] = jnp.zeros(star_total.shape, F32)

    def block(b, _):
        g = load_block(table, pl.multiple_of(b * 8, 8))
        star_total[:, 0:STARS] += pull_of(g, [twice(here[c, 0:STARS]) for c in range(3)])
        return 0

    lax.fori_loop(0, CELL_BLOCKS, block, 0, unroll=4)
    mine = by_group([cells[k : k + 1] for k in range(4)])
    g = jnp.concatenate([*table_rows(*mine), jnp.zeros((1, LANES), F32)], axis=0)
    star_total[:, 0:STARS] += pull_of(g, [here[c, 0:STARS] for c in range(3)])
    summed = add_parts(star_total[:, 0:STARS])
    p = jnp.concatenate([own[0:1, 0:STARS], own[0:1, 64 : 64 + STARS], own[1:2, 0:STARS]], axis=0)
    cell_out[...] = summed[3:6] - p * summed[6:7]


def correct_kernel(pos, vel, acc, jerk, parts, cell, first, second, pos_out, vel_out, gal_out):
    gal_out[:, 0 : 2 * LEAF] = first[...]
    gal_out[:, 2 * LEAF : 4 * LEAF] = second[...]
    summed = parts[0] + parts[1] + parts[2] + parts[3]
    new_acc = summed[0:3, 0:STARS] + cell[...]
    new_jerk = summed[3:6, 0:STARS]
    new_vel = (
        vel[...]
        + TIME_STEP * 0.5 * (acc[...] + new_acc)
        + STEP_SQ / 12.0 * (jerk[...] - new_jerk)
    )
    vel_out[...] = new_vel
    pos_out[...] = (
        pos[...]
        + TIME_STEP * 0.5 * (vel[...] + new_vel)
        + STEP_SQ / 12.0 * (acc[...] - new_acc)
    )


def shape(*lengths):
    return jax.ShapeDtypeStruct(lengths, F32)


VMEM_SPEC = pl.BlockSpec(memory_space=pltpu.VMEM)
PARAMS = pltpu.CompilerParams(vmem_limit_bytes=32 * 1024 * 1024)


def call(kernel, out_shape, scratch=(), scalars=0, work=0):
    def run(*operands):
        return pl.pallas_call(
            kernel,
            out_shape=out_shape,
            in_specs=[pl.BlockSpec(memory_space=pltpu.SMEM)] * scalars + [VMEM_SPEC] * (len(operands) - scalars),
            out_specs=jax.tree.map(lambda _: VMEM_SPEC, out_shape),
            scratch_shapes=[pltpu.VMEM(lengths, kind) for lengths, kind in scratch],
            compiler_params=PARAMS,
            cost_estimate=pl.CostEstimate(flops=work, bytes_accessed=400_000, transcendentals=work // 40),
        )(*operands)

    return run


def exchange(x, axis):
    return lax.all_to_all(x, axis, split_axis=0, concat_axis=0, tiled=True)


def body(
    star_pos, star_vel, star_mass, star_acc, star_jerk, gal_pos, gal_vel, gal_mass, group_of, let_send, star_leaf
):
    masses = gal_mass.reshape(1, -1)
    star_rows, own, cells, send = call(
        prepare_kernel, (shape(N_NARROW, 8, LANES), shape(8, LANES), shape(8, LANES), shape(N_Z, 8, LANES))
    )(
        star_pos,
        star_vel,
        star_acc,
        star_jerk,
        star_mass.reshape(1, -1),
        gal_pos,
        masses,
        group_of.reshape(1, -1),
        let_send.reshape(1, -1),
    )
    arrived = exchange(send, Z)
    onward = call(onward_kernel, shape(N_XY, 80, LANES))(arrived.reshape(N_Z * 8, LANES))
    stars = exchange(onward, XY)
    stars, star_rows = lax.optimization_barrier((stars, star_rows))
    siblings = exchange(star_rows, NARROW)
    n_targets = N_NARROW * STARS
    leaf_scratch = [((3, 2 * LEAF, LANES), F32), ((32, 2 * LEAF), F32)]
    gal_first, table = call(
        first_pull_kernel,
        (shape(3, 2 * LEAF), shape(2, 8 * BLOCKS, LANES)),
        [((64 * 8, LANES), F32)] + leaf_scratch,
        scalars=1,
        work=30_000_000,
    )(star_leaf, gal_pos, gal_vel, masses, stars)
    later_stars, table = lax.optimization_barrier((stars, table))
    partial = call(
        hermite_kernel,
        shape(N_NARROW, 8, LANES),
        [
            ((2, 16 * 32, LANES), F32),
            ((n_targets, 64), BF16),
            ((3, n_targets, LANES), F32),
            ((32, n_targets), F32),
            ((3, n_targets, LANES), F32),
        ],
        work=80_000_000,
    )(siblings, later_stars)
    shared = exchange(partial, NARROW)
    gal_second, cell_acc = call(
        second_pull_kernel,
        (shape(3, 2 * LEAF), shape(3, STARS)),
        leaf_scratch + [((32, LANES), F32)],
        work=30_000_000,
    )(gal_pos, gal_vel, own, cells, table)
    star_pos_new, star_vel_new, gal_vel_new = call(
        correct_kernel, (shape(3, STARS), shape(3, STARS), shape(3, 4 * LEAF))
    )(star_pos, star_vel, star_acc, star_jerk, shared, cell_acc, gal_first, gal_second)
    return gal_vel_new, star_pos_new, star_vel_new


def solution(mesh):
    torus = Mesh(mesh.devices.reshape(N_Z, N_XY, N_NARROW), ALL)
    cols = P(None, ALL)
    return jax.shard_map(
        body,
        mesh=torus,
        in_specs=(
            cols,
            cols,
            P(ALL),
            cols,
            cols,
            cols,
            cols,
            P(ALL),
            P(ALL),
            P(ALL, None, None),
            P(ALL, None),
        ),
        out_specs=(cols, cols, cols),
        check_vma=False,
    )
```

time: 87.1 us -> 77.8 us (0.89)
  Pallas kernels: 27.5 us -> 21.4 us
  waiting for transfers between devices: 4.54 us -> 0.01 us
  local copies, waits for them, and re-layouts: 2.2 us -> 4.11 us
  starting transfers between devices: 13.7 us -> 12.6 us
    pallas_call x4 -> x6, Pallas kernels: 27.5 us -> 21.4 us  [run(): pl.pallas_call(kernel, out_shape=out_shape, in_specs=[pl.BlockSpec(memory...]
    all_to_all x2, waiting for transfers between devices: 4.54 us -> 0.01 us  [exchange(): return lax.all_to_all(x, axis, split_axis=0, concat_axis=0, tiled=True)]
    unnamed x23 -> x28, local copies, waits for them, and re-layouts: 1.36 us -> 4.11 us
    all_to_all x2, starting transfers between devices: 13.7 us -> 12.6 us  [exchange(): return lax.all_to_all(x, axis, split_axis=0, concat_axis=0, tiled=True)]
  transfers between devices with their start and end apart: 2 -> 2, of which waited for: 1 -> 0; matrix products, arithmetic and copies ran while one was open for 1% -> 0% of each run, Pallas kernels for 13% -> 14%
where the time goes in v2:
time: 77.8 us; the launch traced here: 77.3 us
  blocking collectives  38.4 us (49%)
  Pallas kernels  21.4 us (28%)
  starting transfers between devices  12.6 us (16%)
  local copies, waits for them, and re-layouts  4.11 us (5%)
    all_to_all x2, blocking collectives, exchange(): return lax.all_to_all(x, axis, split_axis=0, concat_axis=0, tiled=True)  38.4 us
    pallas_call x6, Pallas kernels, run(): pl.pallas_call(kernel, out_shape=out_shape, in_specs=[pl.BlockSpec(memory...  21.4 us
    all_to_all x2, starting transfers between devices, exchange(): return lax.all_to_all(x, axis, split_axis=0, concat_axis=0, tiled=True)  12.6 us
    unnamed x28, local copies, waits for them, and re-layouts  4.11 us
  transfers between devices with their start and end apart: 2, of which 0 were waited for; matrix products, arithmetic and copies ran while one was open for 0% of the time, Pallas kernels for 14%

profile of v2, /device:TPU:1, one launch (start us, length us, event | category | flops | bytes accessed | tf_op | source)
XLA Modules:
  0.0 77.3 jit_solution(3079330950149143394)
XLA Ops:
  0.6 0.0 copy-start.4
  0.7 0.6 copy-done.4
  1.3 0.0 copy-done.3
  1.3 0.0 copy-done.2
  1.3 0.0 copy-done.10
  1.4 0.7 copy-done
  2.1 0.7 copy-done.5
  2.7 0.7 copy-done.7
  3.4 0.7 copy-done.8
  4.1 0.7 shard_map.130
  4.8 27.1 %all_to_all.20 = f32[16,8,128]{2,1,0:T(8,128)S(1)} all-to-all(f32[16,8,128]{2,1,0:T(8,128)S(1)} %get-tuple-element.18), channel_id=1, replica_groups=mesh['wide_z'=16,'wide_xy'=8,'narrow'=4] {'wide_z'}, dimensions={0} | all-to-all | bytes 131072 | tf_op jit(solution)/shard_map/all_to_all | solution.py:372
  31.9 0.1 shard_map.131
  32.0 11.3 %all_to_all.21.stars = f32[8,80,128]{2,1,0:T(8,128)S(1)} all-to-all(f32[8,80,128]{2,1,0:T(8,128)S(1)} %shard_map.131), channel_id=1, replica_groups=mesh['wide_z'=16,'wide_xy'=8,'narrow'=4] {'wide_xy'}, dimensions={0} | all-to-all | bytes 655360 | tf_op jit(solution)/shard_map/all_to_all | solution.py:372
  43.4 7.9 %all-to-all-start.2 = ((f32[4,8,128]{2,1,0:T(8,128)}), f32[4,8,128]{2,1,0:T(8,128)S(1)}, u32[]{:S(2)}, u32[]{:S(2)}) async-start(f32[4,8,128]{2,1,0:T(8,128)} %get-tuple-element.20), calls=%async_computation.2 | async-start | bytes 32768 | tf_op jit(solution)/shard_map/all_to_all | solution.py:372
  51.2 0.0 copy-done.12
  51.2 5.2 %shard_map.132 = (f32[3,256]{1,0:T(4,128)S(1)}, f32[2,208,128]{2,1,0:T(8,128)S(1)}) custom-call(s32[4,8]{1,0:T(4,128)S(1)} %copy-done.13, f32[3,512]{1,0:T(4,128)S(1)} %copy-done.1, f32[3,512]{1,0:T(4,128)S(1)} %copy-done.12, f32[1,512]{1,0:T(1,128)S(1)} %bitcast.8, f32[8,80,128]{2,1,0:T(8,128)S(1)} %all_to_all.21.stars), custom_call_target="tpu_custom_call" | custom-call | flops 30000000 | bytes 400000 | tf_op jit(solution)/shard_map/pallas_call | solution.py:358
  56.4 0.0 all-to-all-done.2.sib
  56.4 9.2 %shard_map.133 = f32[4,8,128]{2,1,0:T(8,128)} custom-call(f32[4,8,128]{2,1,0:T(8,128)S(1)} %all-to-all-done.2.sib, f32[8,80,128]{2,1,0:T(8,128)S(1)} %all_to_all.21.stars), custom_call_target="tpu_custom_call" | custom-call | flops 80000000 | bytes 400000 | tf_op jit(solution)/shard_map/pallas_call | solution.py:358
  65.6 4.8 %all-to-all-start.3 = ((f32[4,8,128]{2,1,0:T(8,128)}), f32[4,8,128]{2,1,0:T(8,128)S(1)}, u32[]{:S(2)}, u32[]{:S(2)}) async-start(f32[4,8,128]{2,1,0:T(8,128)} %shard_map.133), calls=%async_computation.3 | async-start | bytes 32768 | tf_op jit(solution)/shard_map/all_to_all | solution.py:372
  70.4 5.6 %shard_map.134 = (f32[3,256]{1,0:T(4,128)S(1)}, f32[3,64]{1,0:T(4,128)S(1)}) custom-call(f32[3,512]{1,0:T(4,128)S(1)} %copy-done.1, f32[3,512]{1,0:T(4,128)S(1)} %copy-done.12, f32[8,128]{1,0:T(8,128)S(1)} %get-tuple-element.24.own, f32[8,128]{1,0:T(8,128)S(1)} %get-tuple-element.25.cells, f32[2,208,128]{2,1,0:T(8,128)S(1)} %get-tuple-element.26.table), custom_call_target="tpu_custom_call" | custom-call | flops 30000000 | bytes 400000 | tf_op jit(solution)/shard_map/pallas_call | solution.py:358
  76.0 0.0 all-to-all-done.3.parts
  76.0 0.0 copy-start.6
  76.0 0.7 copy-done.6
  76.7 0.6 shard_map.135
  (16 shorter events, 0.0 us)
Async XLA Ops:
  0.6 0.7 copy-start.4
  0.6 0.7 copy-start.3
  0.7 0.7 copy-start.2
  0.7 0.7 copy-start.10
  0.7 0.7 copy-start.11
  1.4 0.7 copy-start
  2.0 0.7 copy-start.5
  2.7 0.7 copy-start.7
  3.4 0.7 copy-start.8
  43.4 7.9 %copy-start.1 = (f32[3,512]{1,0:T(4,128)S(1)}, f32[3,512]{1,0:T(4,128)}, u32[]{:S(2)}) copy-start(f32[3,512]{1,0:T(4,128)} %gpos.5) | copy-start | bytes 18436
  43.4 7.9 %copy-start.9 = (f32[512]{0:T(512)S(1)}, f32[512]{0:T(512)}, u32[]{:S(2)}) copy-start(f32[512]{0:T(512)} %param.18) | copy-start | bytes 6148
  43.4 7.9 %copy-start.12 = (f32[3,512]{1,0:T(4,128)S(1)}, f32[3,512]{1,0:T(4,128)}, u32[]{:S(2)}) copy-start(f32[3,512]{1,0:T(4,128)} %gvel.3) | copy-start | bytes 18436
  43.4 7.9 %copy-start.13 = (s32[4,8]{1,0:T(4,128)S(1)}, s32[4,8]{1,0:T(4,128)}, u32[]{:S(2)}) copy-start(s32[4,8]{1,0:T(4,128)} %leaf_ref.1) | copy-start | bytes 388
  43.4 13.0 %all-to-all-start.2 = ((f32[4,8,128]{2,1,0:T(8,128)}), f32[4,8,128]{2,1,0:T(8,128)S(1)}, u32[]{:S(2)}, u32[]{:S(2)}) async-start(f32[4,8,128]{2,1,0:T(8,128)} %get-tuple-element.20), calls=%async_computation.2 | async-start | bytes 32768 | tf_op jit(solution)/shard_map/all_to_all | solution.py:372
  65.6 10.4 %all-to-all-start.3 = ((f32[4,8,128]{2,1,0:T(8,128)}), f32[4,8,128]{2,1,0:T(8,128)S(1)}, u32[]{:S(2)}, u32[]{:S(2)}) async-start(f32[4,8,128]{2,1,0:T(8,128)} %shard_map.133), calls=%async_computation.3 | async-start | bytes 32768 | tf_op jit(solution)/shard_map/all_to_all | solution.py:372
  76.0 0.7 copy-start.6

commit v3 on v2

--- a/solution.py
+++ b/solution.py
@@ -30,7 +30,17 @@
     return pred_pos, pred_vel
 
 
-def prepare_kernel(pos, vel, acc, jerk, mass, gpos, gmass, group, let, star_out, own_out, cells_out, send_out):
+def prepare_kernel(*refs):
+    sources, outs, held, done = refs[:9], refs[9:13], refs[13:22], refs[22]
+    own_out, cells_out, send_out, state_out = outs
+    copies = [pltpu.make_async_copy(sources[k], held[k], done.at[k]) for k in range(9)]
+    for copy in copies:
+        copy.start()
+    for copy in copies:
+        copy.wait()
+    pos, vel, acc, jerk, mass, gpos, gmass, group, let = held
+    for k, ref in enumerate((pos, vel, acc, jerk)):
+        state_out[k] = ref[...]
     pred_pos, pred_vel = predict(pos[...], vel[...], acc[...], jerk[...])
     zero = jnp.zeros((1, STARS), F32)
     rows = [
@@ -40,10 +50,7 @@
         (mass[...], zero),
     ]
     packed = jnp.concatenate([jnp.concatenate(pair, axis=1) for pair in rows], axis=0)
-    own = jnp.concatenate([packed, jnp.zeros((4, LANES), F32)], axis=0)
-    own_out[...] = own
-    for n in range(N_NARROW):
-        star_out[n] = own
+    own_out[...] = jnp.concatenate([packed, jnp.zeros((4, LANES), F32)], axis=0)
     leaf_rows = []
     for leaf in range(4):
         span = pl.ds(leaf * LEAF, LEAF)
@@ -153,7 +160,7 @@
     return jnp.concatenate([ref[half, pl.ds(at, 8), :] for half in range(2)], axis=1)
 
 
-def hermite_kernel(sib, stars, out, table, slots, here, main, drag):
+def hermite_kernel(own, near, middle, far, stars, out, table, slots, here, main, drag):
     n_targets = N_NARROW * STARS
     x, y = star_plane_pair(stars, 0)
     z, u = star_plane_pair(stars, 1)
@@ -166,7 +173,7 @@
         store_rows(table, 16, 8 + row, plane)
     comps = [[] for _ in range(6)]
     for n in range(N_NARROW):
-        block = sib[n]
+        block = (own, near, middle, far)[n][...]
         for c in range(6):
             comps[c].append(block[c // 2 : c // 2 + 1, 64 * (c % 2) : 64 * (c % 2) + 64])
     rows = [jnp.concatenate(parts, axis=1) for parts in comps]
@@ -204,8 +211,10 @@
     dragged = jnp.concatenate([row_sums(drag[c]) for c in range(3)], axis=0)
     jerk = total[3:6] - q * total[6:7] - 3.0 * dragged
     both = jnp.concatenate([accel, jerk, jnp.zeros((2, n_targets), F32)], axis=0)
+    me = lax.axis_index(NARROW)
     for n in range(N_NARROW):
-        out[n, :, 0:STARS] = both[:, n * STARS : (n + 1) * STARS]
+        owner = lax.rem(me + (N_NARROW - n), N_NARROW)
+        out[owner, :, 0:STARS] = both[:, n * STARS : (n + 1) * STARS]
 
 
 CELL_BLOCKS = 16
@@ -273,75 +282,72 @@
     return weighted(block, inv * (inv * inv))
 
 
-def pull_leaves(first, gpos, gvel, table, here, total, gal_out):
-    count = 2 * LEAF
-    span = slice(first * LEAF, first * LEAF + count)
-    p = gpos[:, span]
-    turned = jnp.transpose(jnp.concatenate([p, jnp.zeros((5, count), F32)], axis=0))
-    for c in range(3):
-        here[c, 0:count] = jnp.broadcast_to(turned[:, c : c + 1], (count, LANES))
-    total[...] = jnp.zeros(total.shape, F32)
-
-    def block(b, _):
-        g = load_block(table, pl.multiple_of(b * 8, 8))
-        total[...] += pull_of(g, [twice(here[c, 0:count]) for c in range(3)])
-        return 0
-
-    lax.fori_loop(0, STAR_BLOCK, block, 0, unroll=3)
-    for k in range(2):
-        lanes = slice(k * LEAF, (k + 1) * LEAF)
-        for half in range(2):
-            at = 8 * (STAR_BLOCK + 2 * (first + k) + half)
-            total[:, lanes] += pull_of(load_block(table, at), [twice(here[c, lanes]) for c in range(3)])
-    summed = add_parts(total[...])
-    gal_out[...] = gvel[:, span] + TIME_STEP * (summed[3:6] - p * summed[6:7])
-
-
-def first_pull_kernel(leaf_ref, gpos, gvel, gmass, stars, gal_out, table, splanes, here, total):
+def pull_kernel(leaf_ref, gpos, gvel, gmass, stars, own, cells, gal_out, cell_out, table, splanes, here, total):
     table[...] = jnp.zeros(table.shape, F32)
     splanes[...] = jnp.zeros(splanes.shape, F32)
     build_table(leaf_ref, gpos, gmass, stars, table, splanes)
-    pull_leaves(0, gpos, gvel, table, here, total, gal_out)
-
-
-def second_pull_kernel(gpos, gvel, own, cells, table, gal_out, cell_out, here, total, star_total):
-    pull_leaves(2, gpos, gvel, table, here, total, gal_out)
-    turned = jnp.transpose(own[...])
+    bodies, half = 4 * LEAF, 2 * LEAF
+    p = gpos[...]
+    turned = jnp.transpose(jnp.concatenate([p, jnp.zeros((5, bodies), F32)], axis=0))
     for c in range(3):
-        column = turned[64 * (c % 2) : 64 * (c % 2) + 64, c // 2 : c // 2 + 1]
-        here[c, 0:STARS] = jnp.broadcast_to(column, (STARS, LANES))
-    star_total[...] = jnp.zeros(star_total.shape, F32)
+        here[c] = jnp.broadcast_to(turned[:, c : c + 1], (bodies, LANES))
+    total[...] = jnp.zeros(total.shape, F32)
 
     def block(b, _):
         g = load_block(table, pl.multiple_of(b * 8, 8))
-        star_total[:, 0:STARS] += pull_of(g, [twice(here[c, 0:STARS]) for c in range(3)])
+        for first in (0, half):
+            spot = slice(first, first + half)
+            total[:, spot] += pull_of(g, [twice(here[c, spot]) for c in range(3)])
         return 0
 
-    lax.fori_loop(0, CELL_BLOCKS, block, 0, unroll=4)
-    mine = by_group([cells[k : k + 1] for k in range(4)])
-    g = jnp.concatenate([*table_rows(*mine), jnp.zeros((1, LANES), F32)], axis=0)
-    star_total[:, 0:STARS] += pull_of(g, [here[c, 0:STARS] for c in range(3)])
-    summed = add_parts(star_total[:, 0:STARS])
-    p = jnp.concatenate([own[0:1, 0:STARS], own[0:1, 64 : 64 + STARS], own[1:2, 0:STARS]], axis=0)
-    cell_out[...] = summed[3:6] - p * summed[6:7]
-
-
-def correct_kernel(pos, vel, acc, jerk, parts, cell, first, second, pos_out, vel_out, gal_out):
-    gal_out[:, 0 : 2 * LEAF] = first[...]
-    gal_out[:, 2 * LEAF : 4 * LEAF] = second[...]
+    lax.fori_loop(0, STAR_BLOCK, block, 0, unroll=2)
+    for leaf in range(4):
+        spot = slice(leaf * LEAF, (leaf + 1) * LEAF)
+        for k in range(2):
+            g = load_block(table, 8 * (STAR_BLOCK + 2 * leaf + k))
+            total[:, spot] += pull_of(g, [twice(here[c, spot]) for c in range(3)])
+    summed = add_parts(total[...])
+    gal_out[...] = gvel[...] + TIME_STEP * (summed[3:6] - p * summed[6:7])
+
+    turned = jnp.transpose(own[...])
+    at = [
+        jnp.broadcast_to(turned[64 * (c % 2) : 64 * (c % 2) + 64, c // 2 : c // 2 + 1], (STARS, LANES))
+        for c in range(3)
+    ]
+
+    def add_pull(source, sums):
+        dx, dy, dz = [source[c] - at[c] for c in range(3)]
+        inv = lax.rsqrt(dx * dx + (dy * dy + (dz * dz + SOFT_SQ)))
+        weight = source[3] * inv * (inv * inv)
+        return sums[0] + weight * dx, sums[1] + weight * dy, sums[2] + weight * dz
+
+    def row(b, sums):
+        for side in range(2):
+            sums = add_pull([table[side, pl.ds(b * 8 + r, 1), :] for r in (0, 1, 2, 6)], sums)
+        return sums
+
+    zero = jnp.zeros((STARS, LANES), F32)
+    res = add_pull(by_group([cells[k : k + 1] for k in range(4)]), (zero,) * 3)
+    res = lax.fori_loop(0, CELL_BLOCKS, row, res, unroll=2)
+    for c in range(3):
+        cell_out[c : c + 1] = row_sums(res[c])
+
+
+def correct_kernel(state, parts, cell, pos_out, vel_out):
+    pos, vel, acc, jerk = [state[k] for k in range(4)]
     summed = parts[0] + parts[1] + parts[2] + parts[3]
     new_acc = summed[0:3, 0:STARS] + cell[...]
     new_jerk = summed[3:6, 0:STARS]
     new_vel = (
-        vel[...]
-        + TIME_STEP * 0.5 * (acc[...] + new_acc)
-        + STEP_SQ / 12.0 * (jerk[...] - new_jerk)
+        vel
+        + TIME_STEP * 0.5 * (acc + new_acc)
+        + STEP_SQ / 12.0 * (jerk - new_jerk)
     )
     vel_out[...] = new_vel
     pos_out[...] = (
-        pos[...]
-        + TIME_STEP * 0.5 * (vel[...] + new_vel)
-        + STEP_SQ / 12.0 * (acc[...] - new_acc)
+        pos
+        + TIME_STEP * 0.5 * (vel + new_vel)
+        + STEP_SQ / 12.0 * (acc - new_acc)
     )
 
 
@@ -350,18 +356,17 @@
 
 
 VMEM_SPEC = pl.BlockSpec(memory_space=pltpu.VMEM)
-PARAMS = pltpu.CompilerParams(vmem_limit_bytes=32 * 1024 * 1024)
-
-
-def call(kernel, out_shape, scratch=(), scalars=0, work=0):
+
+
+def call(kernel, out_shape, scratch=(), scalars=0, work=0, space=VMEM_SPEC, extra=(), limit=32 * 1024 * 1024):
     def run(*operands):
         return pl.pallas_call(
             kernel,
             out_shape=out_shape,
-            in_specs=[pl.BlockSpec(memory_space=pltpu.SMEM)] * scalars + [VMEM_SPEC] * (len(operands) - scalars),
+            in_specs=[pl.BlockSpec(memory_space=pltpu.SMEM)] * scalars + [space] * (len(operands) - scalars),
             out_specs=jax.tree.map(lambda _: VMEM_SPEC, out_shape),
-            scratch_shapes=[pltpu.VMEM(lengths, kind) for lengths, kind in scratch],
-            compiler_params=PARAMS,
+            scratch_shapes=[pltpu.VMEM(lengths, kind) for lengths, kind in scratch] + list(extra),
+            compiler_params=pltpu.CompilerParams(vmem_limit_bytes=limit),
             cost_estimate=pl.CostEstimate(flops=work, bytes_accessed=400_000, transcendentals=work // 40),
         )(*operands)
 
@@ -376,9 +381,7 @@
     star_pos, star_vel, star_mass, star_acc, star_jerk, gal_pos, gal_vel, gal_mass, group_of, let_send, star_leaf
 ):
     masses = gal_mass.reshape(1, -1)
-    star_rows, own, cells, send = call(
-        prepare_kernel, (shape(N_NARROW, 8, LANES), shape(8, LANES), shape(8, LANES), shape(N_Z, 8, LANES))
-    )(
+    operands = (
         star_pos,
         star_vel,
         star_acc,
@@ -389,21 +392,22 @@
         group_of.reshape(1, -1),
         let_send.reshape(1, -1),
     )
+    own, cells, send, state = call(
+        prepare_kernel,
+        (shape(8, LANES), shape(8, LANES), shape(N_Z, 8, LANES), shape(4, 3, STARS)),
+        [(x.shape, x.dtype) for x in operands],
+        space=pl.BlockSpec(memory_space=pltpu.HBM),
+        extra=[pltpu.SemaphoreType.DMA((len(operands),))],
+        limit=None,
+    )(*operands)
     arrived = exchange(send, Z)
     onward = call(onward_kernel, shape(N_XY, 80, LANES))(arrived.reshape(N_Z * 8, LANES))
     stars = exchange(onward, XY)
-    stars, star_rows = lax.optimization_barrier((stars, star_rows))
-    siblings = exchange(star_rows, NARROW)
+    siblings = [
+        lax.ppermute(own, NARROW, [(n, (n + k) % N_NARROW) for n in range(N_NARROW)])
+        for k in range(1, N_NARROW)
+    ]
     n_targets = N_NARROW * STARS
-    leaf_scratch = [((3, 2 * LEAF, LANES), F32), ((32, 2 * LEAF), F32)]
-    gal_first, table = call(
-        first_pull_kernel,
-        (shape(3, 2 * LEAF), shape(2, 8 * BLOCKS, LANES)),
-        [((64 * 8, LANES), F32)] + leaf_scratch,
-        scalars=1,
-        work=30_000_000,
-    )(star_leaf, gal_pos, gal_vel, masses, stars)
-    later_stars, table = lax.optimization_barrier((stars, table))
     partial = call(
         hermite_kernel,
         shape(N_NARROW, 8, LANES),
@@ -415,17 +419,23 @@
             ((3, n_targets, LANES), F32),
         ],
         work=80_000_000,
-    )(siblings, later_stars)
+    )(own, *siblings, stars)
     shared = exchange(partial, NARROW)
-    gal_second, cell_acc = call(
-        second_pull_kernel,
-        (shape(3, 2 * LEAF), shape(3, STARS)),
-        leaf_scratch + [((32, LANES), F32)],
-        work=30_000_000,
-    )(gal_pos, gal_vel, own, cells, table)
-    star_pos_new, star_vel_new, gal_vel_new = call(
-        correct_kernel, (shape(3, STARS), shape(3, STARS), shape(3, 4 * LEAF))
-    )(star_pos, star_vel, star_acc, star_jerk, shared, cell_acc, gal_first, gal_second)
+    gal_vel_new, cell_acc = call(
+        pull_kernel,
+        (shape(3, 4 * LEAF), shape(3, STARS)),
+        [
+            ((2, 8 * BLOCKS, LANES), F32),
+            ((64 * 8, LANES), F32),
+            ((3, 4 * LEAF, LANES), F32),
+            ((32, 4 * LEAF), F32),
+        ],
+        scalars=1,
+        work=60_000_000,
+    )(star_leaf, gal_pos, gal_vel, masses, stars, own, cells)
+    star_pos_new, star_vel_new = call(correct_kernel, (shape(3, STARS), shape(3, STARS)))(
+        state, shared, cell_acc
+    )
     return gal_vel_new, star_pos_new, star_vel_new
 
 

time: 77.8 us -> 76.2 us (0.979)
  blocking collectives: 38.4 us -> 27.3 us
  starting transfers between devices: 12.6 us -> 20.6 us
  waiting for transfers between devices: 0.01 us -> 4.45 us
  local copies, waits for them, and re-layouts: 4.11 us -> 0.03 us
  Pallas kernels: 21.4 us -> 22.5 us
    all_to_all x2 -> x1, blocking collectives: 38.4 us -> 27.3 us  [exchange(): return lax.all_to_all(x, axis, split_axis=0, concat_axis=0, tiled=True)]
    ppermute x0 -> x3, starting transfers between devices: none -> 11 us  [body(): lax.ppermute(own, NARROW, [(n, (n + k) % N_NARROW) for n in range(N_NARRO...]
    ppermute x0 -> x3, waiting for transfers between devices: none -> 4.45 us  [body(): lax.ppermute(own, NARROW, [(n, (n + k) % N_NARROW) for n in range(N_NARRO...]
    unnamed x28 -> x14, local copies, waits for them, and re-layouts: 4.11 us -> 0.03 us
    all_to_all x2, starting transfers between devices: 12.6 us -> 9.59 us  [exchange(): return lax.all_to_all(x, axis, split_axis=0, concat_axis=0, tiled=True)]
    pallas_call x6 -> x5, Pallas kernels: 21.4 us -> 22.5 us  [run(): pl.pallas_call(kernel, out_shape=out_shape, in_specs=[pl.BlockSpec(memory...]
  transfers between devices with their start and end apart: 2 -> 5, of which waited for: 0 -> 2; matrix products, arithmetic and copies ran while one was open for 0% -> 0% of each run, Pallas kernels for 14% -> 13%
where the time goes in v3:
time: 76.2 us; the launch traced here: 75.6 us
  blocking collectives  27.3 us (36%)
  Pallas kernels  22.5 us (30%)
  starting transfers between devices  20.6 us (27%)
  waiting for transfers between devices  4.45 us (6%)
    all_to_all x1, blocking collectives, exchange(): return lax.all_to_all(x, axis, split_axis=0, concat_axis=0, tiled=True)  27.3 us
    pallas_call x5, Pallas kernels, run(): pl.pallas_call(kernel, out_shape=out_shape, in_specs=[pl.BlockSpec(memory...  22.5 us
    ppermute x3, starting transfers between devices, body(): lax.ppermute(own, NARROW, [(n, (n + k) % N_NARROW) for n in range(N_NARRO...  11 us
    all_to_all x2, starting transfers between devices, exchange(): return lax.all_to_all(x, axis, split_axis=0, concat_axis=0, tiled=True)  9.59 us
    ppermute x3, waiting for transfers between devices, body(): lax.ppermute(own, NARROW, [(n, (n + k) % N_NARROW) for n in range(N_NARRO...  4.45 us
  transfers between devices with their start and end apart: 5, of which 2 were waited for; matrix products, arithmetic and copies ran while one was open for 0% of the time, Pallas kernels for 13%

profile of v3, /device:TPU:1, one launch (start us, length us, event | category | flops | bytes accessed | tf_op | source)
XLA Modules:
  0.0 75.6 jit_solution(1457281311050818572)
XLA Ops:
  0.6 1.8 %shard_map.130 = (f32[8,128]{1,0:T(8,128)}, f32[8,128]{1,0:T(8,128)}, f32[16,8,128]{2,1,0:T(8,128)}, f32[4,3,64]{2,1,0:T(4,128)}) custom-call(f32[3,64]{1,0:T(4,128)} %refs_0_.1, f32[3,64]{1,0:T(4,128)} %refs_1_.1, f32[3,64]{1,0:T(4,128)} %refs_2_.1, f32[3,64]{1,0:T(4,128)} %refs_3_.1, f32[1,64]{1,0:T(1,128)} %bitcast.9, f32[3,512]{1,0:T(4,128)} %gpos.1, ...), custom_call_target="tpu_custom_call" | custom-call | bytes 400000 | tf_op jit(solution)/shard_map/pallas_call | solution.py:363
  2.4 27.3 %all_to_all.15 = f32[16,8,128]{2,1,0:T(8,128)S(1)} all-to-all(f32[16,8,128]{2,1,0:T(8,128)} %get-tuple-element.11), channel_id=1, replica_groups=mesh['wide_z'=16,'wide_xy'=8,'narrow'=4] {'wide_z'}, dimensions={0} | all-to-all | bytes 131072 | tf_op jit(solution)/shard_map/all_to_all | solution.py:377
  29.8 0.8 %shard_map.131 = f32[8,80,128]{2,1,0:T(8,128)} custom-call(f32[128,128]{1,0:T(8,128)S(1)} %bitcast.5), custom_call_target="tpu_custom_call" | custom-call | bytes 400000 | tf_op jit(solution)/shard_map/pallas_call | solution.py:363
  30.6 5.2 %all-to-all-start.1 = ((f32[8,80,128]{2,1,0:T(8,128)}), f32[8,80,128]{2,1,0:T(8,128)S(1)}, u32[]{:S(2)}, u32[]{:S(2)}) async-start(f32[8,80,128]{2,1,0:T(8,128)} %shard_map.131), calls=%async_computation.1 | async-start | bytes 655360 | tf_op jit(solution)/shard_map/all_to_all | solution.py:377
  35.8 0.0 copy-done.4
  35.8 6.8 %collective-permute-start = (f32[8,128]{1,0:T(8,128)S(1)}, f32[8,128]{1,0:T(8,128)S(1)}, u32[]{:S(2)}, u32[]{:S(2)}) collective-permute-start(f32[8,128]{1,0:T(8,128)S(1)} %copy-done.4), channel_id=1, source_target_pairs={{0,1},{1,2},{2,3},{3,0},{4,5},{5,6},{6,7},{7,4},{8,9},{9,10},{10,1... | collective-permute-start | bytes 12296 | tf_op jit(solution)/shard_map/ppermute | solution.py:407
  42.6 2.3 %collective-permute-start.1 = (f32[8,128]{1,0:T(8,128)S(1)}, f32[8,128]{1,0:T(8,128)S(1)}, u32[]{:S(2)}, u32[]{:S(2)}) collective-permute-start(f32[8,128]{1,0:T(8,128)S(1)} %copy-done.4), channel_id=1, source_target_pairs={{0,2},{1,3},{2,0},{3,1},{4,6},{5,7},{6,4},{7,5},{8,10},{9,11},{10,... | collective-permute-start | bytes 12296 | tf_op jit(solution)/shard_map/ppermute | solution.py:407
  44.8 2.0 %collective-permute-start.2 = (f32[8,128]{1,0:T(8,128)S(1)}, f32[8,128]{1,0:T(8,128)S(1)}, u32[]{:S(2)}, u32[]{:S(2)}) collective-permute-start(f32[8,128]{1,0:T(8,128)S(1)} %copy-done.4), channel_id=1, source_target_pairs={{0,3},{1,0},{2,1},{3,2},{4,7},{5,4},{6,5},{7,6},{8,11},{9,8},{10,9... | collective-permute-start | bytes 12296 | tf_op jit(solution)/shard_map/ppermute | solution.py:407
  46.8 0.0 collective-permute-done.near
  46.8 1.6 %collective-permute-done.1.middle = f32[8,128]{1,0:T(8,128)S(1)} collective-permute-done((f32[8,128]{1,0:T(8,128)S(1)}, f32[8,128]{1,0:T(8,128)S(1)}, u32[]{:S(2)}, u32[]{:S(2)}) %collective-permute-start.1) | collective-permute-done | bytes 4128 | tf_op jit(solution)/shard_map/ppermute | solution.py:407
  48.4 2.8 %collective-permute-done.2.far = f32[8,128]{1,0:T(8,128)S(1)} collective-permute-done((f32[8,128]{1,0:T(8,128)S(1)}, f32[8,128]{1,0:T(8,128)S(1)}, u32[]{:S(2)}, u32[]{:S(2)}) %collective-permute-start.2) | collective-permute-done | bytes 4128 | tf_op jit(solution)/shard_map/ppermute | solution.py:407
  51.3 0.0 all-to-all-done.1.stars
  51.3 9.2 %shard_map.133 = f32[4,8,128]{2,1,0:T(8,128)} custom-call(f32[8,128]{1,0:T(8,128)S(1)} %copy-done.4, f32[8,128]{1,0:T(8,128)S(1)} %collective-permute-done.near, f32[8,128]{1,0:T(8,128)S(1)} %collective-permute-done.1.middle, f32[8,128]{1,0:T(8,128)S(1)} %collective-permute-done.2.far, f32[8,80,128]{2,1,0:T(8,128)S(1)} %all-to-all-done.1.stars), custom_call_target="tpu_custom_call" | custom-call | flops 80000000 | bytes 400000 | tf_op jit(solution)/shard_map/pallas_call | solution.py:363
  60.5 0.0 copy-start.6
  60.5 4.4 %all-to-all-start.2 = ((f32[4,8,128]{2,1,0:T(8,128)}), f32[4,8,128]{2,1,0:T(8,128)S(1)}, u32[]{:S(2)}, u32[]{:S(2)}) async-start(f32[4,8,128]{2,1,0:T(8,128)} %shard_map.133), calls=%async_computation.2 | async-start | bytes 32768 | tf_op jit(solution)/shard_map/all_to_all | solution.py:377
  64.9 0.0 copy-done
  64.9 0.0 copy-done.2
  64.9 0.0 copy-done.3
  64.9 0.0 copy-done.5
  64.9 0.0 copy-done.6
  65.0 0.0 copy-start.1
  65.0 10.1 %shard_map.132 = (f32[3,512]{1,0:T(4,128)}, f32[3,64]{1,0:T(4,128)S(1)}) custom-call(s32[4,8]{1,0:T(4,128)S(1)} %copy-done.6, f32[3,512]{1,0:T(4,128)S(1)} %copy-done, f32[3,512]{1,0:T(4,128)S(1)} %copy-done.3, f32[1,512]{1,0:T(1,128)S(1)} %bitcast.7, f32[8,80,128]{2,1,0:T(8,128)S(1)} %all-to-all-done.1.stars, f32[8,128]{1,0:T(8,128)S(1)} %copy-done.4, ...), custom_call_target="tpu_custom_call" | custom-call | flops 60000000 | bytes 400000 | tf_op jit(solution)/shard_map/pallas_call | solution.py:363
  75.0 0.0 all-to-all-done.2.parts
  75.1 0.6 shard_map.134
  (6 shorter events, 0.0 us)
Async XLA Ops:
  30.6 5.2 %copy-start.4 = (f32[8,128]{1,0:T(8,128)S(1)}, f32[8,128]{1,0:T(8,128)}, u32[]{:S(2)}) copy-start(f32[8,128]{1,0:T(8,128)} %get-tuple-element.12.own) | copy-start | bytes 12292
  30.6 20.7 %all-to-all-start.1 = ((f32[8,80,128]{2,1,0:T(8,128)}), f32[8,80,128]{2,1,0:T(8,128)S(1)}, u32[]{:S(2)}, u32[]{:S(2)}) async-start(f32[8,80,128]{2,1,0:T(8,128)} %shard_map.131), calls=%async_computation.1 | async-start | bytes 655360 | tf_op jit(solution)/shard_map/all_to_all | solution.py:377
  35.8 11.1 %collective-permute-start = (f32[8,128]{1,0:T(8,128)S(1)}, f32[8,128]{1,0:T(8,128)S(1)}, u32[]{:S(2)}, u32[]{:S(2)}) collective-permute-start(f32[8,128]{1,0:T(8,128)S(1)} %copy-done.4), channel_id=1, source_target_pairs={{0,1},{1,2},{2,3},{3,0},{4,5},{5,6},{6,7},{7,4},{8,9},{9,10},{10,1... | collective-permute-start | bytes 12296 | tf_op jit(solution)/shard_map/ppermute | solution.py:407
  42.6 5.9 %collective-permute-start.1 = (f32[8,128]{1,0:T(8,128)S(1)}, f32[8,128]{1,0:T(8,128)S(1)}, u32[]{:S(2)}, u32[]{:S(2)}) collective-permute-start(f32[8,128]{1,0:T(8,128)S(1)} %copy-done.4), channel_id=1, source_target_pairs={{0,2},{1,3},{2,0},{3,1},{4,6},{5,7},{6,4},{7,5},{8,10},{9,11},{10,... | collective-permute-start | bytes 12296 | tf_op jit(solution)/shard_map/ppermute | solution.py:407
  44.8 6.4 %collective-permute-start.2 = (f32[8,128]{1,0:T(8,128)S(1)}, f32[8,128]{1,0:T(8,128)S(1)}, u32[]{:S(2)}, u32[]{:S(2)}) collective-permute-start(f32[8,128]{1,0:T(8,128)S(1)} %copy-done.4), channel_id=1, source_target_pairs={{0,3},{1,0},{2,1},{3,2},{4,7},{5,4},{6,5},{7,6},{8,11},{9,8},{10,9... | collective-permute-start | bytes 12296 | tf_op jit(solution)/shard_map/ppermute | solution.py:407
  60.5 4.5 %copy-start = (f32[3,512]{1,0:T(4,128)S(1)}, f32[3,512]{1,0:T(4,128)}, u32[]{:S(2)}) copy-start(f32[3,512]{1,0:T(4,128)} %gpos.1) | copy-start | bytes 18436
  60.5 4.5 %copy-start.2 = (f32[512]{0:T(512)S(1)}, f32[512]{0:T(512)}, u32[]{:S(2)}) copy-start(f32[512]{0:T(512)} %param.18) | copy-start | bytes 6148
  60.5 4.5 %copy-start.3 = (f32[3,512]{1,0:T(4,128)S(1)}, f32[3,512]{1,0:T(4,128)}, u32[]{:S(2)}) copy-start(f32[3,512]{1,0:T(4,128)} %gvel.1) | copy-start | bytes 18436
  60.5 4.5 %copy-start.5 = (f32[8,128]{1,0:T(8,128)S(1)}, f32[8,128]{1,0:T(8,128)}, u32[]{:S(2)}) copy-start(f32[8,128]{1,0:T(8,128)} %get-tuple-element.13.cells) | copy-start | bytes 12292
  60.5 4.5 %copy-start.6 = (s32[4,8]{1,0:T(4,128)S(1)}, s32[4,8]{1,0:T(4,128)}, u32[]{:S(2)}) copy-start(s32[4,8]{1,0:T(4,128)} %leaf_ref.1) | copy-start | bytes 388
  60.5 14.6 %all-to-all-start.2 = ((f32[4,8,128]{2,1,0:T(8,128)}), f32[4,8,128]{2,1,0:T(8,128)S(1)}, u32[]{:S(2)}, u32[]{:S(2)}) async-start(f32[4,8,128]{2,1,0:T(8,128)} %shard_map.133), calls=%async_computation.2 | async-start | bytes 32768 | tf_op jit(solution)/shard_map/all_to_all | solution.py:377
  65.0 10.1 %copy-start.1 = (f32[4,3,64]{2,1,0:T(4,128)S(1)}, f32[4,3,64]{2,1,0:T(4,128)}, u32[]{:S(2)}) copy-start(f32[4,3,64]{2,1,0:T(4,128)} %get-tuple-element.15.state) | copy-start | bytes 9220

commit v4 on v3

--- a/solution.py
+++ b/solution.py
@@ -401,12 +401,13 @@
         limit=None,
     )(*operands)
     arrived = exchange(send, Z)
-    onward = call(onward_kernel, shape(N_XY, 80, LANES))(arrived.reshape(N_Z * 8, LANES))
-    stars = exchange(onward, XY)
     siblings = [
         lax.ppermute(own, NARROW, [(n, (n + k) % N_NARROW) for n in range(N_NARROW)])
         for k in range(1, N_NARROW)
     ]
+    arrived, *siblings = lax.optimization_barrier((arrived, *siblings))
+    onward = call(onward_kernel, shape(N_XY, 80, LANES))(arrived.reshape(N_Z * 8, LANES))
+    stars = exchange(onward, XY)
     n_targets = N_NARROW * STARS
     partial = call(
         hermite_kernel,

time: 76.2 us -> 69.8 us (0.916)
  blocking collectives: 27.3 us -> 10.4 us
  starting transfers between devices: 20.6 us -> 35.5 us
  waiting for transfers between devices: 4.45 us -> 0.72 us
    all_to_all x1, blocking collectives: 27.3 us -> 10.4 us  [exchange(): return lax.all_to_all(x, axis, split_axis=0, concat_axis=0, tiled=True)]
    all_to_all x2, starting transfers between devices: 9.59 us -> 23.4 us  [exchange(): return lax.all_to_all(x, axis, split_axis=0, concat_axis=0, tiled=True)]
    ppermute x3, waiting for transfers between devices: 4.45 us -> 0.72 us  [body(): lax.ppermute(own, NARROW, [(n, (n + k) % N_NARROW) for n in range(N_NARRO...]
    ppermute x3, starting transfers between devices: 11 us -> 12.2 us  [body(): lax.ppermute(own, NARROW, [(n, (n + k) % N_NARROW) for n in range(N_NARRO...]
  transfers between devices with their start and end apart: 5 -> 5, of which waited for: 2 -> 1; matrix products, arithmetic and copies ran while one was open for 0% -> 0% of each run, Pallas kernels for 13% -> 15%
where the time goes in v4:
time: 69.8 us; the launch traced here: 69.3 us
  starting transfers between devices  35.5 us (51%)
  Pallas kernels  21.8 us (31%)
  blocking collectives  10.4 us (15%)
  between operations  0.75 us (1%)
  waiting for transfers between devices  0.72 us (1%)
    all_to_all x2, starting transfers between devices, exchange(): return lax.all_to_all(x, axis, split_axis=0, concat_axis=0, tiled=True)  23.4 us
    pallas_call x5, Pallas kernels, run(): pl.pallas_call(kernel, out_shape=out_shape, in_specs=[pl.BlockSpec(memory...  21.8 us
    ppermute x3, starting transfers between devices, body(): lax.ppermute(own, NARROW, [(n, (n + k) % N_NARROW) for n in range(N_NARRO...  12.2 us
    all_to_all x1, blocking collectives, exchange(): return lax.all_to_all(x, axis, split_axis=0, concat_axis=0, tiled=True)  10.4 us
  transfers between devices with their start and end apart: 5, of which 1 were waited for; matrix products, arithmetic and copies ran while one was open for 0% of the time, Pallas kernels for 15%

profile of v4, /device:TPU:1, one launch (start us, length us, event | category | flops | bytes accessed | tf_op | source)
XLA Modules:
  0.0 69.3 jit_solution(13355542507337766765)
XLA Ops:
  0.6 1.8 %shard_map.130 = (f32[8,128]{1,0:T(8,128)}, f32[8,128]{1,0:T(8,128)}, f32[16,8,128]{2,1,0:T(8,128)}, f32[4,3,64]{2,1,0:T(4,128)}) custom-call(f32[3,64]{1,0:T(4,128)} %refs_0_.1, f32[3,64]{1,0:T(4,128)} %refs_1_.1, f32[3,64]{1,0:T(4,128)} %refs_2_.1, f32[3,64]{1,0:T(4,128)} %refs_3_.1, f32[1,64]{1,0:T(1,128)} %bitcast.9, f32[3,512]{1,0:T(4,128)} %gpos.1, ...), custom_call_target="tpu_custom_call" | custom-call | bytes 400000 | tf_op jit(solution)/shard_map/pallas_call | solution.py:363
  2.4 0.0 copy-start.4
  2.5 15.8 %all-to-all-start = ((f32[16,8,128]{2,1,0:T(8,128)}), f32[16,8,128]{2,1,0:T(8,128)S(1)}, u32[]{:S(2)}, u32[]{:S(2)}) async-start(f32[16,8,128]{2,1,0:T(8,128)} %get-tuple-element.15), calls=%async_computation | async-start | bytes 131072 | tf_op jit(solution)/shard_map/all_to_all | solution.py:377
  18.2 0.0 copy-done.4
  18.2 2.9 %collective-permute-start.2 = (f32[8,128]{1,0:T(8,128)S(1)}, f32[8,128]{1,0:T(8,128)S(1)}, u32[]{:S(2)}, u32[]{:S(2)}) collective-permute-start(f32[8,128]{1,0:T(8,128)S(1)} %copy-done.4), channel_id=1, source_target_pairs={{0,3},{1,0},{2,1},{3,2},{4,7},{5,4},{6,5},{7,6},{8,11},{9,8},{10,9... | collective-permute-start | bytes 12296 | tf_op jit(solution)/shard_map/ppermute | solution.py:405
  21.1 4.8 %collective-permute-start.1 = (f32[8,128]{1,0:T(8,128)S(1)}, f32[8,128]{1,0:T(8,128)S(1)}, u32[]{:S(2)}, u32[]{:S(2)}) collective-permute-start(f32[8,128]{1,0:T(8,128)S(1)} %copy-done.4), channel_id=1, source_target_pairs={{0,2},{1,3},{2,0},{3,1},{4,6},{5,7},{6,4},{7,5},{8,10},{9,11},{10,... | collective-permute-start | bytes 12296 | tf_op jit(solution)/shard_map/ppermute | solution.py:405
  25.9 4.5 %collective-permute-start = (f32[8,128]{1,0:T(8,128)S(1)}, f32[8,128]{1,0:T(8,128)S(1)}, u32[]{:S(2)}, u32[]{:S(2)}) collective-permute-start(f32[8,128]{1,0:T(8,128)S(1)} %copy-done.4), channel_id=1, source_target_pairs={{0,1},{1,2},{2,3},{3,0},{4,5},{5,6},{6,7},{7,4},{8,9},{9,10},{10,1... | collective-permute-start | bytes 12296 | tf_op jit(solution)/shard_map/ppermute | solution.py:405
  30.4 0.0 collective-permute-done.2.far
  30.4 0.0 collective-permute-done.1.middle
  30.4 0.7 %collective-permute-done.near = f32[8,128]{1,0:T(8,128)S(1)} collective-permute-done((f32[8,128]{1,0:T(8,128)S(1)}, f32[8,128]{1,0:T(8,128)S(1)}, u32[]{:S(2)}, u32[]{:S(2)}) %collective-permute-start) | collective-permute-done | bytes 4128 | tf_op jit(solution)/shard_map/ppermute | solution.py:405
  31.2 0.0 all-to-all-done
  31.2 0.1 shard_map.131
  31.3 10.4 %all_to_all.15.stars = f32[8,80,128]{2,1,0:T(8,128)S(1)} all-to-all(f32[8,80,128]{2,1,0:T(8,128)S(1)} %shard_map.131), channel_id=1, replica_groups=mesh['wide_z'=16,'wide_xy'=8,'narrow'=4] {'wide_xy'}, dimensions={0} | all-to-all | bytes 655360 | tf_op jit(solution)/shard_map/all_to_all | solution.py:377
  41.7 9.2 %shard_map.133 = f32[4,8,128]{2,1,0:T(8,128)} custom-call(f32[8,128]{1,0:T(8,128)S(1)} %copy-done.4, f32[8,128]{1,0:T(8,128)S(1)} %collective-permute-done.near, f32[8,128]{1,0:T(8,128)S(1)} %collective-permute-done.1.middle, f32[8,128]{1,0:T(8,128)S(1)} %collective-permute-done.2.far, f32[8,80,128]{2,1,0:T(8,128)S(1)} %all_to_all.15.stars), custom_call_target="tpu_custom_call" | custom-call | flops 80000000 | bytes 400000 | tf_op jit(solution)/shard_map/pallas_call | solution.py:363
  50.9 0.0 copy-start.6
  50.9 7.6 %all-to-all-start.2 = ((f32[4,8,128]{2,1,0:T(8,128)}), f32[4,8,128]{2,1,0:T(8,128)S(1)}, u32[]{:S(2)}, u32[]{:S(2)}) async-start(f32[4,8,128]{2,1,0:T(8,128)} %shard_map.133), calls=%async_computation.2 | async-start | bytes 32768 | tf_op jit(solution)/shard_map/all_to_all | solution.py:377
  58.6 0.0 copy-done
  58.6 0.0 copy-done.2
  58.6 0.0 copy-done.3
  58.6 0.0 copy-done.5
  58.6 10.1 %shard_map.132 = (f32[3,512]{1,0:T(4,128)}, f32[3,64]{1,0:T(4,128)S(1)}) custom-call(s32[4,8]{1,0:T(4,128)S(1)} %copy-done.6, f32[3,512]{1,0:T(4,128)S(1)} %copy-done, f32[3,512]{1,0:T(4,128)S(1)} %copy-done.3, f32[1,512]{1,0:T(1,128)S(1)} %bitcast.7, f32[8,80,128]{2,1,0:T(8,128)S(1)} %all_to_all.15.stars, f32[8,128]{1,0:T(8,128)S(1)} %copy-done.4, ...), custom_call_target="tpu_custom_call" | custom-call | flops 60000000 | bytes 400000 | tf_op jit(solution)/shard_map/pallas_call | solution.py:363
  68.7 0.0 all-to-all-done.2.parts
  68.7 0.0 copy-done.1
  68.7 0.6 shard_map.134
  (6 shorter events, 0.0 us)
Async XLA Ops:
  2.4 15.8 %copy-start.4 = (f32[8,128]{1,0:T(8,128)S(1)}, f32[8,128]{1,0:T(8,128)}, u32[]{:S(2)}) copy-start(f32[8,128]{1,0:T(8,128)} %get-tuple-element.16.own) | copy-start | bytes 12292
  2.5 28.7 %all-to-all-start = ((f32[16,8,128]{2,1,0:T(8,128)}), f32[16,8,128]{2,1,0:T(8,128)S(1)}, u32[]{:S(2)}, u32[]{:S(2)}) async-start(f32[16,8,128]{2,1,0:T(8,128)} %get-tuple-element.15), calls=%async_computation | async-start | bytes 131072 | tf_op jit(solution)/shard_map/all_to_all | solution.py:377
  18.2 12.2 %collective-permute-start.2 = (f32[8,128]{1,0:T(8,128)S(1)}, f32[8,128]{1,0:T(8,128)S(1)}, u32[]{:S(2)}, u32[]{:S(2)}) collective-permute-start(f32[8,128]{1,0:T(8,128)S(1)} %copy-done.4), channel_id=1, source_target_pairs={{0,3},{1,0},{2,1},{3,2},{4,7},{5,4},{6,5},{7,6},{8,11},{9,8},{10,9... | collective-permute-start | bytes 12296 | tf_op jit(solution)/shard_map/ppermute | solution.py:405
  21.1 9.3 %collective-permute-start.1 = (f32[8,128]{1,0:T(8,128)S(1)}, f32[8,128]{1,0:T(8,128)S(1)}, u32[]{:S(2)}, u32[]{:S(2)}) collective-permute-start(f32[8,128]{1,0:T(8,128)S(1)} %copy-done.4), channel_id=1, source_target_pairs={{0,2},{1,3},{2,0},{3,1},{4,6},{5,7},{6,4},{7,5},{8,10},{9,11},{10,... | collective-permute-start | bytes 12296 | tf_op jit(solution)/shard_map/ppermute | solution.py:405
  25.9 5.2 %collective-permute-start = (f32[8,128]{1,0:T(8,128)S(1)}, f32[8,128]{1,0:T(8,128)S(1)}, u32[]{:S(2)}, u32[]{:S(2)}) collective-permute-start(f32[8,128]{1,0:T(8,128)S(1)} %copy-done.4), channel_id=1, source_target_pairs={{0,1},{1,2},{2,3},{3,0},{4,5},{5,6},{6,7},{7,4},{8,9},{9,10},{10,1... | collective-permute-start | bytes 12296 | tf_op jit(solution)/shard_map/ppermute | solution.py:405
  50.9 7.6 %copy-start = (f32[3,512]{1,0:T(4,128)S(1)}, f32[3,512]{1,0:T(4,128)}, u32[]{:S(2)}) copy-start(f32[3,512]{1,0:T(4,128)} %gpos.1) | copy-start | bytes 18436
  50.9 7.6 %copy-start.2 = (f32[512]{0:T(512)S(1)}, f32[512]{0:T(512)}, u32[]{:S(2)}) copy-start(f32[512]{0:T(512)} %param.18) | copy-start | bytes 6148
  50.9 7.6 %copy-start.3 = (f32[3,512]{1,0:T(4,128)S(1)}, f32[3,512]{1,0:T(4,128)}, u32[]{:S(2)}) copy-start(f32[3,512]{1,0:T(4,128)} %gvel.1) | copy-start | bytes 18436
  50.9 7.7 %copy-start.5 = (f32[8,128]{1,0:T(8,128)S(1)}, f32[8,128]{1,0:T(8,128)}, u32[]{:S(2)}) copy-start(f32[8,128]{1,0:T(8,128)} %get-tuple-element.18.cells) | copy-start | bytes 12292
  50.9 7.7 %copy-start.6 = (s32[4,8]{1,0:T(4,128)S(1)}, s32[4,8]{1,0:T(4,128)}, u32[]{:S(2)}) copy-start(s32[4,8]{1,0:T(4,128)} %leaf_ref.1) | copy-start | bytes 388
  50.9 17.8 %all-to-all-start.2 = ((f32[4,8,128]{2,1,0:T(8,128)}), f32[4,8,128]{2,1,0:T(8,128)S(1)}, u32[]{:S(2)}, u32[]{:S(2)}) async-start(f32[4,8,128]{2,1,0:T(8,128)} %shard_map.133), calls=%async_computation.2 | async-start | bytes 32768 | tf_op jit(solution)/shard_map/all_to_all | solution.py:377
  58.6 10.1 %copy-start.1 = (f32[4,3,64]{2,1,0:T(4,128)S(1)}, f32[4,3,64]{2,1,0:T(4,128)}, u32[]{:S(2)}) copy-start(f32[4,3,64]{2,1,0:T(4,128)} %get-tuple-element.20.state) | copy-start | bytes 9220

commit v5 on v3

--- a/solution.py
+++ b/solution.py
@@ -22,6 +22,7 @@
 STARS = 64
 STAR_ROWS = 4
 PER_BLOCK = 2 * LANES
+CHUNK_BLOCKS = N_Z * STARS // PER_BLOCK
 
 
 def predict(pos, vel, acc, jerk):
@@ -75,7 +76,7 @@
         send_out[z] = jnp.concatenate([packed[0:3], last] + leaf_rows, axis=0)
 
 
-def onward_kernel(arrived, out):
+def onward_kernel(arrived, out, mine):
     flat = arrived
     for pair in range(N_Z // 2):
         both = jnp.concatenate(
@@ -91,21 +92,27 @@
         for leaf in range(4):
             rows = jnp.where(which == float(leaf), cells[leaf], rows)
         out[e, 64:80, :] = rows
+    mine[...] = out[lax.axis_index(XY)]
 
 
 def low_lanes(shape):
     return lax.broadcasted_iota(jnp.int32, shape, 1) < 64
 
 
-def star_plane_pair(stars, r):
-    low = low_lanes((N_XY // 2 * N_Z, LANES))
-    picked = [stars[e, pl.ds(r, N_Z, stride=STAR_ROWS), :] for e in range(N_XY)]
-    first = jnp.concatenate(picked[: N_XY // 2], axis=0)
-    second = jnp.concatenate(picked[N_XY // 2 :], axis=0)
+def star_plane_pair(chunks, r):
+    picked = [chunk[pl.ds(r, N_Z, stride=STAR_ROWS), :] for chunk in chunks]
+    first = jnp.concatenate([rows[: N_Z // 2] for rows in picked], axis=0)
+    second = jnp.concatenate([rows[N_Z // 2 :] for rows in picked], axis=0)
+    low = low_lanes(first.shape)
     return (
         jnp.where(low, first, pltpu.roll(second, 64, 1)),
         jnp.where(low, pltpu.roll(first, 64, 1), second),
     )
+
+
+def other_chunks(stars):
+    me = lax.axis_index(XY)
+    return [stars.at[lax.rem(me + k, N_XY)] for k in range(1, N_XY)]
 
 
 def row_sums(x):
@@ -160,12 +167,12 @@
     return jnp.concatenate([ref[half, pl.ds(at, 8), :] for half in range(2)], axis=1)
 
 
-def hermite_kernel(own, near, middle, far, stars, out, table, slots, here, main, drag):
+def hermite_partial(own, beside, across, chunks, table, slots, here, main, drag):
     n_targets = N_NARROW * STARS
-    x, y = star_plane_pair(stars, 0)
-    z, u = star_plane_pair(stars, 1)
-    v, w = star_plane_pair(stars, 2)
-    m, _ = star_plane_pair(stars, 3)
+    x, y = star_plane_pair(chunks, 0)
+    z, u = star_plane_pair(chunks, 1)
+    v, w = star_plane_pair(chunks, 2)
+    m, _ = star_plane_pair(chunks, 3)
     product = m * (x * u + y * v + z * w)
     for row, plane in enumerate((x, y, z)):
         store_rows(table, 16, row, plane)
@@ -173,7 +180,7 @@
         store_rows(table, 16, 8 + row, plane)
     comps = [[] for _ in range(6)]
     for n in range(N_NARROW):
-        block = (own, near, middle, far)[n][...]
+        block = (own[...], beside[...], across[0:8], across[8:16])[n]
         for c in range(6):
             comps[c].append(block[c // 2 : c // 2 + 1, 64 * (c % 2) : 64 * (c % 2) + 64])
     rows = [jnp.concatenate(parts, axis=1) for parts in comps]
@@ -205,22 +212,29 @@
             drag[c] += term[:, 0:LANES] + term[:, LANES:PER_BLOCK]
         return 0
 
-    lax.fori_loop(0, table.shape[1] // 16, block, 0, unroll=4)
+    lax.fori_loop(0, CHUNK_BLOCKS * len(chunks), block, 0, unroll=4)
     total = add_parts(main[...])
     accel = total[0:3] - p * total[6:7]
     dragged = jnp.concatenate([row_sums(drag[c]) for c in range(3)], axis=0)
     jerk = total[3:6] - q * total[6:7] - 3.0 * dragged
     both = jnp.concatenate([accel, jerk, jnp.zeros((2, n_targets), F32)], axis=0)
+    return both
+
+
+def early_hermite_kernel(own, beside, across, mine, out, *scratch):
+    out[...] = hermite_partial(own, beside, across, [mine], *scratch)
+
+
+def hermite_kernel(own, beside, across, early, stars, out, *scratch):
+    both = early[...] + hermite_partial(own, beside, across, other_chunks(stars), *scratch)
     me = lax.axis_index(NARROW)
     for n in range(N_NARROW):
-        owner = lax.rem(me + (N_NARROW - n), N_NARROW)
+        owner = me ^ n
         out[owner, :, 0:STARS] = both[:, n * STARS : (n + 1) * STARS]
 
 
-CELL_BLOCKS = 16
-BODY_BLOCK = 16
-STAR_BLOCK = 18
-BLOCKS = 26
+EARLY_CELLS, BODY_BLOCK, EARLY_BLOCKS = 2, 2, 4
+CELL_BLOCKS, STAR_BLOCK, BLOCKS = 14, 14, 22
 
 
 def by_group(picked):
@@ -239,23 +253,30 @@
     return (x, y, z, m * x, m * y, m * z, m)
 
 
-def build_table(leaf_ref, gpos, gmass, stars, table, splanes):
-    quarter = N_XY // 4
+def cell_table(chunks, table):
+    rows = [[chunk[64 + 8 * half : 72 + 8 * half, :] for half in range(2)] for chunk in chunks]
     parts = [
-        jnp.concatenate([stars[e, 64:80, :] for e in range(quarter * k, quarter * (k + 1))], axis=0)
+        jnp.concatenate([pair[k // 2][4 * (k % 2) : 4 * (k % 2) + 4] for pair in rows], axis=0)
         for k in range(4)
     ]
     for row, plane in enumerate(table_rows(*by_group(parts))):
         store_rows(table, 8, row, plane)
+
+
+def body_table(gpos, gmass, table):
     for half in range(2):
         spot = slice(8 * (BODY_BLOCK + half), 8 * (BODY_BLOCK + half) + 7)
         for side in range(2):
             span = slice(half * PER_BLOCK + side * LANES, half * PER_BLOCK + (side + 1) * LANES)
             m = gmass[:, span]
             table[side, spot, :] = jnp.concatenate([gpos[:, span], gpos[:, span] * m, m], axis=0)
-    x, y = star_plane_pair(stars, 0)
-    z, _ = star_plane_pair(stars, 1)
-    m, _ = star_plane_pair(stars, 3)
+
+
+def star_table(leaf_ref, chunks, table, splanes):
+    x, y = star_plane_pair(chunks, 0)
+    z, _ = star_plane_pair(chunks, 1)
+    m, _ = star_plane_pair(chunks, 3)
+    me = lax.axis_index(XY)
     for c, plane in enumerate((x, y, z, m)):
         splanes[pl.ds(c, 64, stride=8), :] = plane
     low = low_lanes((8, LANES))
@@ -264,9 +285,11 @@
             sides = []
             for side in range(2):
                 b = leaf_ref[leaf, 2 * pair + side]
-                place = (b % N_XY) * N_Z + b // N_XY
-                upper = place // 64
-                rows = splanes[pl.ds(pl.multiple_of((place - 64 * upper) * 8, 8), 8), :]
+                chunk = lax.rem(b % N_XY - me + (N_XY - 1) + N_XY, N_XY)
+                z_at = b // N_XY
+                upper = z_at // (N_Z // 2)
+                at = chunk * (N_Z // 2) + z_at - upper * (N_Z // 2)
+                rows = splanes[pl.ds(pl.multiple_of(at * 8, 8), 8), :]
                 sides.append(jnp.where(upper == side, rows, pltpu.roll(rows, 64, 1)))
             rows = jnp.where(low, sides[0], sides[1])
             m = rows[3:4]
@@ -282,16 +305,14 @@
     return weighted(block, inv * (inv * inv))
 
 
-def pull_kernel(leaf_ref, gpos, gvel, gmass, stars, own, cells, gal_out, cell_out, table, splanes, here, total):
-    table[...] = jnp.zeros(table.shape, F32)
-    splanes[...] = jnp.zeros(splanes.shape, F32)
-    build_table(leaf_ref, gpos, gmass, stars, table, splanes)
-    bodies, half = 4 * LEAF, 2 * LEAF
-    p = gpos[...]
-    turned = jnp.transpose(jnp.concatenate([p, jnp.zeros((5, bodies), F32)], axis=0))
+def spread_bodies(gpos, here):
+    turned = jnp.transpose(jnp.concatenate([gpos[...], jnp.zeros((5, 4 * LEAF), F32)], axis=0))
     for c in range(3):
-        here[c] = jnp.broadcast_to(turned[:, c : c + 1], (bodies, LANES))
-    total[...] = jnp.zeros(total.shape, F32)
+        here[c] = jnp.broadcast_to(turned[:, c : c + 1], (4 * LEAF, LANES))
+
+
+def pull_all_bodies(table, blocks, unroll, here, total):
+    half = 2 * LEAF
 
     def block(b, _):
         g = load_block(table, pl.multiple_of(b * 8, 8))
@@ -300,37 +321,69 @@
             total[:, spot] += pull_of(g, [twice(here[c, spot]) for c in range(3)])
         return 0
 
-    lax.fori_loop(0, STAR_BLOCK, block, 0, unroll=2)
+    lax.fori_loop(0, blocks, block, 0, unroll=unroll)
+
+
+def body_pull(total, gpos):
+    summed = add_parts(total[...])
+    return summed[3:6] - gpos[...] * summed[6:7]
+
+
+def star_pull(own, table, blocks, more):
+    turned = jnp.transpose(own[...])
+    at = [
+        jnp.broadcast_to(turned[64 * (c % 2) : 64 * (c % 2) + 64, c // 2 : c // 2 + 1], (STARS, LANES))
+        for c in range(3)
+    ]
+
+    def add_pull(source, sums):
+        dx, dy, dz = [source[c] - at[c] for c in range(3)]
+        inv = lax.rsqrt(dx * dx + (dy * dy + (dz * dz + SOFT_SQ)))
+        weight = source[3] * inv * (inv * inv)
+        return sums[0] + weight * dx, sums[1] + weight * dy, sums[2] + weight * dz
+
+    def row(b, sums):
+        for side in range(2):
+            sums = add_pull([table[side, pl.ds(b * 8 + r, 1), :] for r in (0, 1, 2, 6)], sums)
+        return sums
+
+    res = (jnp.zeros((STARS, LANES), F32),) * 3
+    if more is not None:
+        res = add_pull(more, res)
+    res = lax.fori_loop(0, blocks, row, res, unroll=2)
+    return jnp.concatenate([row_sums(part) for part in res], axis=0)
+
+
+def early_pull_kernel(gpos, gmass, own, cells, mine, gal_out, cell_out, table, here, total):
+    table[...] = jnp.zeros(table.shape, F32)
+    cell_table([mine], table)
+    body_table(gpos, gmass, table)
+    spread_bodies(gpos, here)
+    total[...] = jnp.zeros(total.shape, F32)
+    pull_all_bodies(table, EARLY_BLOCKS, 2, here, total)
+    gal_out[...] = body_pull(total, gpos)
+    leaf_cells = by_group([cells[k : k + 1] for k in range(4)])
+    cell_out[...] = star_pull(own, table, EARLY_CELLS, leaf_cells)
+
+
+def pull_kernel(
+    leaf_ref, gpos, gvel, stars, own, early_gal, early_cell, gal_out, cell_out, table, splanes, here, total
+):
+    table[...] = jnp.zeros(table.shape, F32)
+    splanes[...] = jnp.zeros(splanes.shape, F32)
+    others = other_chunks(stars)
+    cell_table(others, table)
+    star_table(leaf_ref, others + [stars.at[lax.axis_index(XY)]], table, splanes)
+    spread_bodies(gpos, here)
+    total[...] = jnp.zeros(total.shape, F32)
+    pull_all_bodies(table, CELL_BLOCKS, 2, here, total)
     for leaf in range(4):
         spot = slice(leaf * LEAF, (leaf + 1) * LEAF)
         for k in range(2):
             g = load_block(table, 8 * (STAR_BLOCK + 2 * leaf + k))
             total[:, spot] += pull_of(g, [twice(here[c, spot]) for c in range(3)])
-    summed = add_parts(total[...])
-    gal_out[...] = gvel[...] + TIME_STEP * (summed[3:6] - p * summed[6:7])
-
-    turned = jnp.transpose(own[...])
-    at = [
-        jnp.broadcast_to(turned[64 * (c % 2) : 64 * (c % 2) + 64, c // 2 : c // 2 + 1], (STARS, LANES))
-        for c in range(3)
-    ]
-
-    def add_pull(source, sums):
-        dx, dy, dz = [source[c] - at[c] for c in range(3)]
-        inv = lax.rsqrt(dx * dx + (dy * dy + (dz * dz + SOFT_SQ)))
-        weight = source[3] * inv * (inv * inv)
-        return sums[0] + weight * dx, sums[1] + weight * dy, sums[2] + weight * dz
-
-    def row(b, sums):
-        for side in range(2):
-            sums = add_pull([table[side, pl.ds(b * 8 + r, 1), :] for r in (0, 1, 2, 6)], sums)
-        return sums
-
-    zero = jnp.zeros((STARS, LANES), F32)
-    res = add_pull(by_group([cells[k : k + 1] for k in range(4)]), (zero,) * 3)
-    res = lax.fori_loop(0, CELL_BLOCKS, row, res, unroll=2)
-    for c in range(3):
-        cell_out[c : c + 1] = row_sums(res[c])
+    gal_out[...] = gvel[...] + TIME_STEP * (early_gal[...] + body_pull(total, gpos))
+    cell_out[...] = early_cell[...] + star_pull(own, table, CELL_BLOCKS, None)
 
 
 def correct_kernel(state, parts, cell, pos_out, vel_out):
@@ -401,38 +454,46 @@
         limit=None,
     )(*operands)
     arrived = exchange(send, Z)
-    onward = call(onward_kernel, shape(N_XY, 80, LANES))(arrived.reshape(N_Z * 8, LANES))
+    beside = lax.ppermute(own, NARROW, [(n, n ^ 1) for n in range(N_NARROW)])
+    across = lax.ppermute(jnp.concatenate([own, beside]), NARROW, [(n, n ^ 2) for n in range(N_NARROW)])
+    arrived, beside, across = lax.optimization_barrier((arrived, beside, across))
+    onward, mine = call(onward_kernel, (shape(N_XY, 80, LANES), shape(80, LANES)))(
+        arrived.reshape(N_Z * 8, LANES)
+    )
     stars = exchange(onward, XY)
-    siblings = [
-        lax.ppermute(own, NARROW, [(n, (n + k) % N_NARROW) for n in range(N_NARROW)])
-        for k in range(1, N_NARROW)
-    ]
     n_targets = N_NARROW * STARS
-    partial = call(
-        hermite_kernel,
-        shape(N_NARROW, 8, LANES),
-        [
-            ((2, 16 * 32, LANES), F32),
+    body_scratch = [((3, 4 * LEAF, LANES), F32), ((32, 4 * LEAF), F32)]
+    early_gal, early_cell = call(
+        early_pull_kernel,
+        (shape(3, 4 * LEAF), shape(3, STARS)),
+        [((2, 8 * (EARLY_BLOCKS + 8), LANES), F32), *body_scratch],
+        work=15_000_000,
+    )(gal_pos, masses, own, cells, mine)
+
+    def hermite_scratch(blocks):
+        return [
+            ((2, 16 * (blocks + 4), LANES), F32),
             ((n_targets, 64), BF16),
             ((3, n_targets, LANES), F32),
             ((32, n_targets), F32),
             ((3, n_targets, LANES), F32),
-        ],
-        work=80_000_000,
-    )(own, *siblings, stars)
+        ]
+
+    early = call(early_hermite_kernel, shape(8, n_targets), hermite_scratch(4), work=10_000_000)(
+        own, beside, across, mine
+    )
+    early, early_gal, early_cell, stars = lax.optimization_barrier((early, early_gal, early_cell, stars))
+    partial = call(hermite_kernel, shape(N_NARROW, 8, LANES), hermite_scratch(28), work=70_000_000)(
+        own, beside, across, early, stars
+    )
     shared = exchange(partial, NARROW)
     gal_vel_new, cell_acc = call(
         pull_kernel,
         (shape(3, 4 * LEAF), shape(3, STARS)),
-        [
-            ((2, 8 * BLOCKS, LANES), F32),
-            ((64 * 8, LANES), F32),
-            ((3, 4 * LEAF, LANES), F32),
-            ((32, 4 * LEAF), F32),
-        ],
+        [((2, 8 * BLOCKS, LANES), F32), ((64 * 8, LANES), F32), *body_scratch],
         scalars=1,
-        work=60_000_000,
-    )(star_leaf, gal_pos, gal_vel, masses, stars, own, cells)
+        work=50_000_000,
+    )(star_leaf, gal_pos, gal_vel, stars, own, early_gal, early_cell)
     star_pos_new, star_vel_new = call(correct_kernel, (shape(3, STARS), shape(3, STARS)))(
         state, shared, cell_acc
     )

time: 76.2 us -> 67.5 us (0.89)
  blocking collectives: 27.3 us -> 0 us
  starting transfers between devices: 20.6 us -> 36.3 us
  Pallas kernels: 22.5 us -> 24 us
  waiting for transfers between devices: 4.45 us -> 5.93 us
    all_to_all x1 -> x0, blocking collectives: 27.3 us -> none  [exchange(): return lax.all_to_all(x, axis, split_axis=0, concat_axis=0, tiled=True)]
    all_to_all x2 -> x3, starting transfers between devices: 9.59 us -> 28.6 us  [exchange(): return lax.all_to_all(x, axis, split_axis=0, concat_axis=0, tiled=True)]
    all_to_all x2 -> x3, waiting for transfers between devices: 0.01 us -> 3.76 us  [exchange(): return lax.all_to_all(x, axis, split_axis=0, concat_axis=0, tiled=True)]
    ppermute x3 -> x2, starting transfers between devices: 11 us -> 7.67 us  [the longest x1 4.81 us: body(): lax.ppermute(jnp.concatenate([own, beside]), NARROW, [(n, n ^ 2) for n in...]
    ppermute x3 -> x2, waiting for transfers between devices: 4.45 us -> 2.16 us  [the longest x1 1.36 us: body(): lax.ppermute(jnp.concatenate([own, beside]), NARROW, [(n, n ^ 2) for n in...]
    pallas_call x5 -> x7, Pallas kernels: 22.5 us -> 24 us  [run(): pl.pallas_call(kernel, out_shape=out_shape, in_specs=[pl.BlockSpec(memory...]
  transfers between devices with their start and end apart: 5 -> 5, of which waited for: 2 -> 4; matrix products, arithmetic and copies ran while one was open for 0% -> 0% of each run, Pallas kernels for 13% -> 19%
where the time goes in v5:
time: 67.5 us; the launch traced here: 67 us
  starting transfers between devices  36.3 us (54%)
  Pallas kernels  24 us (36%)
  waiting for transfers between devices  5.93 us (9%)
  between operations  0.74 us (1%)
    all_to_all x3, starting transfers between devices, exchange(): return lax.all_to_all(x, axis, split_axis=0, concat_axis=0, tiled=True)  28.6 us
    pallas_call x7, Pallas kernels, run(): pl.pallas_call(kernel, out_shape=out_shape, in_specs=[pl.BlockSpec(memory...  24 us
    ppermute x1, starting transfers between devices, body(): lax.ppermute(jnp.concatenate([own, beside]), NARROW, [(n, n ^ 2) for n in...  4.81 us
    all_to_all x3, waiting for transfers between devices, exchange(): return lax.all_to_all(x, axis, split_axis=0, concat_axis=0, tiled=True)  3.76 us
    ppermute x1, starting transfers between devices, body(): beside = lax.ppermute(own, NARROW, [(n, n ^ 1) for n in range(N_NARROW)])  2.86 us
    ppermute x1, waiting for transfers between devices, body(): lax.ppermute(jnp.concatenate([own, beside]), NARROW, [(n, n ^ 2) for n in...  1.36 us
  transfers between devices with their start and end apart: 5, of which 4 were waited for; matrix products, arithmetic and copies ran while one was open for 0% of the time, Pallas kernels for 19%

profile of v5, /device:TPU:1, one launch (start us, length us, event | category | flops | bytes accessed | tf_op | source)
XLA Modules:
  0.0 67.0 jit_solution(16857759702228704274)
XLA Ops:
  0.6 1.8 %shard_map.130 = (f32[8,128]{1,0:T(8,128)}, f32[8,128]{1,0:T(8,128)}, f32[16,8,128]{2,1,0:T(8,128)}, f32[4,3,64]{2,1,0:T(4,128)}) custom-call(f32[3,64]{1,0:T(4,128)} %refs_0_.1, f32[3,64]{1,0:T(4,128)} %refs_1_.1, f32[3,64]{1,0:T(4,128)} %refs_2_.1, f32[3,64]{1,0:T(4,128)} %refs_3_.1, f32[1,64]{1,0:T(1,128)} %bitcast.9, f32[3,512]{1,0:T(4,128)} %gpos.3, ...), custom_call_target="tpu_custom_call" | custom-call | bytes 400000 | tf_op jit(solution)/shard_map/pallas_call | solution.py:416
  2.5 0.0 copy-start.2
  2.5 15.8 %all-to-all-start = ((f32[16,8,128]{2,1,0:T(8,128)}), f32[16,8,128]{2,1,0:T(8,128)S(1)}, u32[]{:S(2)}, u32[]{:S(2)}) async-start(f32[16,8,128]{2,1,0:T(8,128)} %get-tuple-element.23), calls=%async_computation | async-start | bytes 131072 | tf_op jit(solution)/shard_map/all_to_all | solution.py:430
  18.2 0.0 copy-done.2
  18.2 2.9 %collective-permute-start = (f32[8,128]{1,0:T(8,128)S(1)}, f32[8,128]{1,0:T(8,128)S(1)}, u32[]{:S(2)}, u32[]{:S(2)}) collective-permute-start(f32[8,128]{1,0:T(8,128)S(1)} %copy-done.2), channel_id=1, source_target_pairs={{0,1},{1,0},{2,3},{3,2},{4,5},{5,4},{6,7},{7,6},{8,9},{9,8},{10,11... | collective-permute-start | bytes 12296 | tf_op jit(solution)/shard_map/ppermute | solution.py:457
  21.1 0.8 %collective-permute-done.beside = f32[8,128]{1,0:T(8,128)S(1)} collective-permute-done((f32[8,128]{1,0:T(8,128)S(1)}, f32[8,128]{1,0:T(8,128)S(1)}, u32[]{:S(2)}, u32[]{:S(2)}) %collective-permute-start) | collective-permute-done | bytes 4128 | tf_op jit(solution)/shard_map/ppermute | solution.py:457
  21.9 4.8 %collective-permute-start.1 = (f32[16,128]{1,0:T(8,128)S(1)}, f32[16,128]{1,0:T(8,128)S(1)}, u32[]{:S(2)}, u32[]{:S(2)}) collective-permute-start(f32[16,128]{1,0:T(8,128)S(1)} %pad_maximum_fusion), channel_id=1, source_target_pairs={{0,2},{1,3},{2,0},{3,1},{4,6},{5,7},{6,4},{7,5},{8,10},{9,11},{10,... | collective-permute-start | bytes 24584 | tf_op jit(solution)/shard_map/ppermute | solution.py:458
  26.7 1.4 %collective-permute-done.1.across = f32[16,128]{1,0:T(8,128)S(1)} collective-permute-done((f32[16,128]{1,0:T(8,128)S(1)}, f32[16,128]{1,0:T(8,128)S(1)}, u32[]{:S(2)}, u32[]{:S(2)}) %collective-permute-start.1) | collective-permute-done | bytes 8224 | tf_op jit(solution)/shard_map/ppermute | solution.py:458
  28.1 1.7 %all-to-all-done = f32[16,8,128]{2,1,0:T(8,128)S(1)} async-done(((f32[16,8,128]{2,1,0:T(8,128)}), f32[16,8,128]{2,1,0:T(8,128)S(1)}, u32[]{:S(2)}, u32[]{:S(2)}) %all-to-all-start) | async-done | bytes 65568 | tf_op jit(solution)/shard_map/all_to_all | solution.py:430
  29.8 0.8 %shard_map.131 = (f32[8,80,128]{2,1,0:T(8,128)}, f32[80,128]{1,0:T(8,128)S(1)}) custom-call(f32[128,128]{1,0:T(8,128)S(1)} %bitcast.5), custom_call_target="tpu_custom_call" | custom-call | bytes 400000 | tf_op jit(solution)/shard_map/pallas_call | solution.py:416
  30.6 5.0 %all-to-all-start.1 = ((f32[8,80,128]{2,1,0:T(8,128)}), f32[8,80,128]{2,1,0:T(8,128)S(1)}, u32[]{:S(2)}, u32[]{:S(2)}) async-start(f32[8,80,128]{2,1,0:T(8,128)} %get-tuple-element.31), calls=%async_computation.1 | async-start | bytes 655360 | tf_op jit(solution)/shard_map/all_to_all | solution.py:430
  35.7 0.0 copy-start.3
  35.7 0.0 copy-start.5
  35.7 1.7 %shard_map.132.early = f32[8,256]{1,0:T(8,128)S(1)} custom-call(f32[8,128]{1,0:T(8,128)S(1)} %copy-done.2, f32[8,128]{1,0:T(8,128)S(1)} %collective-permute-done.beside, f32[16,128]{1,0:T(8,128)S(1)} %collective-permute-done.1.across, f32[80,128]{1,0:T(8,128)S(1)} %get-tuple-element.27.mine), custom_call_target="tpu_custom_call" | custom-call | flops 10000000 | bytes 400000 | tf_op jit(solution)/shard_map/pallas_call | solution.py:416
  37.3 0.0 copy-done
  37.4 0.0 copy-done.3
  37.4 2.3 %shard_map.133 = (f32[3,512]{1,0:T(4,128)S(1)}, f32[3,64]{1,0:T(4,128)S(1)}) custom-call(f32[3,512]{1,0:T(4,128)S(1)} %copy-done, f32[1,512]{1,0:T(1,128)S(1)} %bitcast.7, f32[8,128]{1,0:T(8,128)S(1)} %copy-done.2, f32[8,128]{1,0:T(8,128)S(1)} %copy-done.5, f32[80,128]{1,0:T(8,128)S(1)} %get-tuple-element.27.mine), custom_call_target="tpu_custom_call" | custom-call | flops 15000000 | bytes 400000 | tf_op jit(solution)/shard_map/pallas_call | solution.py:416
  39.7 2.1 %all-to-all-done.1.stars = f32[8,80,128]{2,1,0:T(8,128)S(1)} async-done(((f32[8,80,128]{2,1,0:T(8,128)}), f32[8,80,128]{2,1,0:T(8,128)S(1)}, u32[]{:S(2)}, u32[]{:S(2)}) %all-to-all-start.1) | async-done | bytes 327712 | tf_op jit(solution)/shard_map/all_to_all | solution.py:430
  41.7 8.2 %shard_map.135 = f32[4,8,128]{2,1,0:T(8,128)} custom-call(f32[8,128]{1,0:T(8,128)S(1)} %copy-done.2, f32[8,128]{1,0:T(8,128)S(1)} %collective-permute-done.beside, f32[16,128]{1,0:T(8,128)S(1)} %collective-permute-done.1.across, f32[8,256]{1,0:T(8,128)S(1)} %shard_map.132.early, f32[8,80,128]{2,1,0:T(8,128)S(1)} %all-to-all-done.1.stars), custom_call_target="tpu_custom_call" | custom-call | flops 70000000 | bytes 400000 | tf_op jit(solution)/shard_map/pallas_call | solution.py:416
  50.0 7.8 %all-to-all-start.2 = ((f32[4,8,128]{2,1,0:T(8,128)}), f32[4,8,128]{2,1,0:T(8,128)S(1)}, u32[]{:S(2)}, u32[]{:S(2)}) async-start(f32[4,8,128]{2,1,0:T(8,128)} %shard_map.135), calls=%async_computation.2 | async-start | bytes 32768 | tf_op jit(solution)/shard_map/all_to_all | solution.py:430
  57.8 8.6 %shard_map.134 = (f32[3,512]{1,0:T(4,128)}, f32[3,64]{1,0:T(4,128)S(1)}) custom-call(s32[4,8]{1,0:T(4,128)S(1)} %copy-done.6, f32[3,512]{1,0:T(4,128)S(1)} %copy-done, f32[3,512]{1,0:T(4,128)S(1)} %copy-done.4, f32[8,80,128]{2,1,0:T(8,128)S(1)} %all-to-all-done.1.stars, f32[8,128]{1,0:T(8,128)S(1)} %copy-done.2, f32[3,512]{1,0:T(4,128)S(1)} %get-tuple-element.33.early_gal, ...), custom_call_target="tpu_custom_call" | custom-call | flops 50000000 | bytes 400000 | tf_op jit(solution)/shard_map/pallas_call | solution.py:416
  66.4 0.0 all-to-all-done.2.parts
  66.4 0.0 copy-done.1
  66.4 0.6 shard_map.136
  (8 shorter events, 0.0 us)
Async XLA Ops:
  2.5 15.8 %copy-start.2 = (f32[8,128]{1,0:T(8,128)S(1)}, f32[8,128]{1,0:T(8,128)}, u32[]{:S(2)}) copy-start(f32[8,128]{1,0:T(8,128)} %get-tuple-element.22.own) | copy-start | bytes 12292
  2.5 27.3 %all-to-all-start = ((f32[16,8,128]{2,1,0:T(8,128)}), f32[16,8,128]{2,1,0:T(8,128)S(1)}, u32[]{:S(2)}, u32[]{:S(2)}) async-start(f32[16,8,128]{2,1,0:T(8,128)} %get-tuple-element.23), calls=%async_computation | async-start | bytes 131072 | tf_op jit(solution)/shard_map/all_to_all | solution.py:430
  18.2 3.7 %collective-permute-start = (f32[8,128]{1,0:T(8,128)S(1)}, f32[8,128]{1,0:T(8,128)S(1)}, u32[]{:S(2)}, u32[]{:S(2)}) collective-permute-start(f32[8,128]{1,0:T(8,128)S(1)} %copy-done.2), channel_id=1, source_target_pairs={{0,1},{1,0},{2,3},{3,2},{4,5},{5,4},{6,7},{7,6},{8,9},{9,8},{10,11... | collective-permute-start | bytes 12296 | tf_op jit(solution)/shard_map/ppermute | solution.py:457
  21.9 6.2 %collective-permute-start.1 = (f32[16,128]{1,0:T(8,128)S(1)}, f32[16,128]{1,0:T(8,128)S(1)}, u32[]{:S(2)}, u32[]{:S(2)}) collective-permute-start(f32[16,128]{1,0:T(8,128)S(1)} %pad_maximum_fusion), channel_id=1, source_target_pairs={{0,2},{1,3},{2,0},{3,1},{4,6},{5,7},{6,4},{7,5},{8,10},{9,11},{10,... | collective-permute-start | bytes 24584 | tf_op jit(solution)/shard_map/ppermute | solution.py:458
  30.6 11.1 %all-to-all-start.1 = ((f32[8,80,128]{2,1,0:T(8,128)}), f32[8,80,128]{2,1,0:T(8,128)S(1)}, u32[]{:S(2)}, u32[]{:S(2)}) async-start(f32[8,80,128]{2,1,0:T(8,128)} %get-tuple-element.31), calls=%async_computation.1 | async-start | bytes 655360 | tf_op jit(solution)/shard_map/all_to_all | solution.py:430
  35.7 1.7 %copy-start = (f32[3,512]{1,0:T(4,128)S(1)}, f32[3,512]{1,0:T(4,128)}, u32[]{:S(2)}) copy-start(f32[3,512]{1,0:T(4,128)} %gpos.3) | copy-start | bytes 18436
  35.7 1.7 %copy-start.3 = (f32[512]{0:T(512)S(1)}, f32[512]{0:T(512)}, u32[]{:S(2)}) copy-start(f32[512]{0:T(512)} %param.18) | copy-start | bytes 6148
  35.7 1.7 %copy-start.5 = (f32[8,128]{1,0:T(8,128)S(1)}, f32[8,128]{1,0:T(8,128)}, u32[]{:S(2)}) copy-start(f32[8,128]{1,0:T(8,128)} %get-tuple-element.28.cells) | copy-start | bytes 12292
  50.0 7.8 %copy-start.4 = (f32[3,512]{1,0:T(4,128)S(1)}, f32[3,512]{1,0:T(4,128)}, u32[]{:S(2)}) copy-start(f32[3,512]{1,0:T(4,128)} %gvel.1) | copy-start | bytes 18436
  50.0 7.8 %copy-start.6 = (s32[4,8]{1,0:T(4,128)S(1)}, s32[4,8]{1,0:T(4,128)}, u32[]{:S(2)}) copy-start(s32[4,8]{1,0:T(4,128)} %leaf_ref.1) | copy-start | bytes 388
  50.0 16.4 %all-to-all-start.2 = ((f32[4,8,128]{2,1,0:T(8,128)}), f32[4,8,128]{2,1,0:T(8,128)S(1)}, u32[]{:S(2)}, u32[]{:S(2)}) async-start(f32[4,8,128]{2,1,0:T(8,128)} %shard_map.135), calls=%async_computation.2 | async-start | bytes 32768 | tf_op jit(solution)/shard_map/all_to_all | solution.py:430
  57.8 8.6 %copy-start.1 = (f32[4,3,64]{2,1,0:T(4,128)S(1)}, f32[4,3,64]{2,1,0:T(4,128)}, u32[]{:S(2)}) copy-start(f32[4,3,64]{2,1,0:T(4,128)} %get-tuple-element.36.state) | copy-start | bytes 9220

commit v6 on v5

--- a/solution.py
+++ b/solution.py
@@ -21,6 +21,7 @@
 N_Z, N_XY, N_NARROW = 16, 8, 4
 STARS = 64
 STAR_ROWS = 4
+CHUNK_ROWS = 72
 PER_BLOCK = 2 * LANES
 CHUNK_BLOCKS = N_Z * STARS // PER_BLOCK
 
@@ -76,38 +77,49 @@
         send_out[z] = jnp.concatenate([packed[0:3], last] + leaf_rows, axis=0)
 
 
+def low_lanes(shape):
+    return lax.broadcasted_iota(jnp.int32, shape, 1) < 64
+
+
+def by_group(picked):
+    lane_group = lax.broadcasted_iota(jnp.int32, picked[0].shape, 1) // GROUPS
+    out = []
+    for c in range(4):
+        plane = picked[c]
+        for k in range(4):
+            if k != c:
+                plane = jnp.where(lane_group == k, pltpu.roll(picked[k], (GROUPS * (k - c)) % LANES, 1), plane)
+        out.append(plane)
+    return out
+
+
 def onward_kernel(arrived, out, mine):
-    flat = arrived
-    for pair in range(N_Z // 2):
-        both = jnp.concatenate(
-            [flat[16 * pair : 16 * pair + 4, :], flat[16 * pair + 8 : 16 * pair + 12, :]], axis=0
+    for r in range(STAR_ROWS):
+        rows = arrived[pl.ds(r, N_Z, stride=8), :]
+        first, second = rows[: N_Z // 2], rows[N_Z // 2 :]
+        low = low_lanes(first.shape)
+        pair = (
+            jnp.where(low, first, pltpu.roll(second, 64, 1)),
+            jnp.where(low, pltpu.roll(first, 64, 1), second),
         )
-        for e in range(N_XY):
-            out[e, 8 * pair : 8 * pair + 8, :] = both
-    ids = flat[pl.ds(3, N_Z, stride=8), :]
-    cells = [flat[pl.ds(4 + leaf, N_Z, stride=8), :] for leaf in range(4)]
+        for side in range(2 if r < STAR_ROWS - 1 else 1):
+            for e in range(N_XY):
+                out[e, 8 * (2 * r + side) : 8 * (2 * r + side) + 8, :] = pair[side]
+    ids = arrived[pl.ds(3, N_Z, stride=8), :]
+    cells = [arrived[pl.ds(4 + leaf, N_Z, stride=8), :] for leaf in range(4)]
     for e in range(N_XY):
         which = jnp.broadcast_to(ids[:, 64 + e : 65 + e], (N_Z, LANES))
         rows = jnp.zeros((N_Z, LANES), F32)
         for leaf in range(4):
             rows = jnp.where(which == float(leaf), cells[leaf], rows)
-        out[e, 64:80, :] = rows
+        planes = by_group([rows[4 * k : 4 * k + 4] for k in range(4)])
+        for half in range(2):
+            out[e, 56 + 8 * half : 64 + 8 * half, :] = jnp.concatenate(planes[2 * half : 2 * half + 2], axis=0)
     mine[...] = out[lax.axis_index(XY)]
 
 
-def low_lanes(shape):
-    return lax.broadcasted_iota(jnp.int32, shape, 1) < 64
-
-
-def star_plane_pair(chunks, r):
-    picked = [chunk[pl.ds(r, N_Z, stride=STAR_ROWS), :] for chunk in chunks]
-    first = jnp.concatenate([rows[: N_Z // 2] for rows in picked], axis=0)
-    second = jnp.concatenate([rows[N_Z // 2 :] for rows in picked], axis=0)
-    low = low_lanes(first.shape)
-    return (
-        jnp.where(low, first, pltpu.roll(second, 64, 1)),
-        jnp.where(low, pltpu.roll(first, 64, 1), second),
-    )
+def star_plane(chunks, c):
+    return jnp.concatenate([chunk[8 * c : 8 * c + 8, :] for chunk in chunks], axis=0)
 
 
 def other_chunks(stars):
@@ -169,10 +181,7 @@
 
 def hermite_partial(own, beside, across, chunks, table, slots, here, main, drag):
     n_targets = N_NARROW * STARS
-    x, y = star_plane_pair(chunks, 0)
-    z, u = star_plane_pair(chunks, 1)
-    v, w = star_plane_pair(chunks, 2)
-    m, _ = star_plane_pair(chunks, 3)
+    x, y, z, u, v, w, m = [star_plane(chunks, c) for c in range(7)]
     product = m * (x * u + y * v + z * w)
     for row, plane in enumerate((x, y, z)):
         store_rows(table, 16, row, plane)
@@ -212,7 +221,7 @@
             drag[c] += term[:, 0:LANES] + term[:, LANES:PER_BLOCK]
         return 0
 
-    lax.fori_loop(0, CHUNK_BLOCKS * len(chunks), block, 0, unroll=4)
+    lax.fori_loop(0, CHUNK_BLOCKS * len(chunks), block, 0, unroll=14 if len(chunks) > 1 else 4)
     total = add_parts(main[...])
     accel = total[0:3] - p * total[6:7]
     dragged = jnp.concatenate([row_sums(drag[c]) for c in range(3)], axis=0)
@@ -237,29 +246,17 @@
 CELL_BLOCKS, STAR_BLOCK, BLOCKS = 14, 14, 22
 
 
-def by_group(picked):
-    lane_group = lax.broadcasted_iota(jnp.int32, picked[0].shape, 1) // GROUPS
-    out = []
-    for c in range(4):
-        plane = picked[c]
-        for k in range(4):
-            if k != c:
-                plane = jnp.where(lane_group == k, pltpu.roll(picked[k], (GROUPS * (k - c)) % LANES, 1), plane)
-        out.append(plane)
-    return out
-
-
 def table_rows(x, y, z, m):
     return (x, y, z, m * x, m * y, m * z, m)
 
 
 def cell_table(chunks, table):
-    rows = [[chunk[64 + 8 * half : 72 + 8 * half, :] for half in range(2)] for chunk in chunks]
-    parts = [
-        jnp.concatenate([pair[k // 2][4 * (k % 2) : 4 * (k % 2) + 4] for pair in rows], axis=0)
-        for k in range(4)
-    ]
-    for row, plane in enumerate(table_rows(*by_group(parts))):
+    planes = []
+    for c in range(4):
+        at = 56 + 8 * (c // 2)
+        rows = [chunk[at : at + 8, :][4 * (c % 2) : 4 * (c % 2) + 4] for chunk in chunks]
+        planes.append(jnp.concatenate(rows, axis=0))
+    for row, plane in enumerate(table_rows(*planes)):
         store_rows(table, 8, row, plane)
 
 
@@ -273,12 +270,9 @@
 
 
 def star_table(leaf_ref, chunks, table, splanes):
-    x, y = star_plane_pair(chunks, 0)
-    z, _ = star_plane_pair(chunks, 1)
-    m, _ = star_plane_pair(chunks, 3)
     me = lax.axis_index(XY)
-    for c, plane in enumerate((x, y, z, m)):
-        splanes[pl.ds(c, 64, stride=8), :] = plane
+    for row, c in enumerate((0, 1, 2, 6)):
+        splanes[pl.ds(row, 64, stride=8), :] = star_plane(chunks, c)
     low = low_lanes((8, LANES))
     for leaf in range(4):
         for pair in range(4):
@@ -350,7 +344,7 @@
     res = (jnp.zeros((STARS, LANES), F32),) * 3
     if more is not None:
         res = add_pull(more, res)
-    res = lax.fori_loop(0, blocks, row, res, unroll=2)
+    res = lax.fori_loop(0, blocks, row, res, unroll=blocks)
     return jnp.concatenate([row_sums(part) for part in res], axis=0)
 
 
@@ -376,7 +370,7 @@
     star_table(leaf_ref, others + [stars.at[lax.axis_index(XY)]], table, splanes)
     spread_bodies(gpos, here)
     total[...] = jnp.zeros(total.shape, F32)
-    pull_all_bodies(table, CELL_BLOCKS, 2, here, total)
+    pull_all_bodies(table, CELL_BLOCKS, CELL_BLOCKS, here, total)
     for leaf in range(4):
         spot = slice(leaf * LEAF, (leaf + 1) * LEAF)
         for k in range(2):
@@ -457,7 +451,7 @@
     beside = lax.ppermute(own, NARROW, [(n, n ^ 1) for n in range(N_NARROW)])
     across = lax.ppermute(jnp.concatenate([own, beside]), NARROW, [(n, n ^ 2) for n in range(N_NARROW)])
     arrived, beside, across = lax.optimization_barrier((arrived, beside, across))
-    onward, mine = call(onward_kernel, (shape(N_XY, 80, LANES), shape(80, LANES)))(
+    onward, mine = call(onward_kernel, (shape(N_XY, CHUNK_ROWS, LANES), shape(CHUNK_ROWS, LANES)))(
         arrived.reshape(N_Z * 8, LANES)
     )
     stars = exchange(onward, XY)

time: 67.5 us -> 65.4 us (0.969)
  Pallas kernels: 24 us -> 22.1 us
    pallas_call x7, Pallas kernels: 24 us -> 22.1 us  [run(): pl.pallas_call(kernel, out_shape=out_shape, in_specs=[pl.BlockSpec(memory...]
  transfers between devices with their start and end apart: 5 -> 5, of which waited for: 4 -> 4; matrix products, arithmetic and copies ran while one was open for 0% -> 0% of each run, Pallas kernels for 19% -> 17%
where the time goes in v6:
time: 65.4 us; the launch traced here: 64.9 us
  starting transfers between devices  36.3 us (56%)
  Pallas kernels  22.1 us (34%)
  waiting for transfers between devices  5.78 us (9%)
  between operations  0.74 us (1%)
    all_to_all x3, starting transfers between devices, exchange(): return lax.all_to_all(x, axis, split_axis=0, concat_axis=0, tiled=True)  28.6 us
    pallas_call x7, Pallas kernels, run(): pl.pallas_call(kernel, out_shape=out_shape, in_specs=[pl.BlockSpec(memory...  22.1 us
    ppermute x1, starting transfers between devices, body(): lax.ppermute(jnp.concatenate([own, beside]), NARROW, [(n, n ^ 2) for n in...  4.81 us
    all_to_all x3, waiting for transfers between devices, exchange(): return lax.all_to_all(x, axis, split_axis=0, concat_axis=0, tiled=True)  3.62 us
    ppermute x1, starting transfers between devices, body(): beside = lax.ppermute(own, NARROW, [(n, n ^ 1) for n in range(N_NARROW)])  2.86 us
    ppermute x1, waiting for transfers between devices, body(): lax.ppermute(jnp.concatenate([own, beside]), NARROW, [(n, n ^ 2) for n in...  1.36 us
  transfers between devices with their start and end apart: 5, of which 4 were waited for; matrix products, arithmetic and copies ran while one was open for 0% of the time, Pallas kernels for 17%

profile of v6, /device:TPU:1, one launch (start us, length us, event | category | flops | bytes accessed | tf_op | source)
XLA Modules:
  0.0 64.9 jit_solution(4646939864376345988)
XLA Ops:
  0.6 1.8 %shard_map.130 = (f32[8,128]{1,0:T(8,128)}, f32[8,128]{1,0:T(8,128)}, f32[16,8,128]{2,1,0:T(8,128)}, f32[4,3,64]{2,1,0:T(4,128)}) custom-call(f32[3,64]{1,0:T(4,128)} %refs_0_.1, f32[3,64]{1,0:T(4,128)} %refs_1_.1, f32[3,64]{1,0:T(4,128)} %refs_2_.1, f32[3,64]{1,0:T(4,128)} %refs_3_.1, f32[1,64]{1,0:T(1,128)} %bitcast.9, f32[3,512]{1,0:T(4,128)} %gpos.3, ...), custom_call_target="tpu_custom_call" | custom-call | bytes 400000 | tf_op jit(solution)/shard_map/pallas_call | solution.py:410
  2.5 0.0 copy-start.2
  2.5 15.8 %all-to-all-start = ((f32[16,8,128]{2,1,0:T(8,128)}), f32[16,8,128]{2,1,0:T(8,128)S(1)}, u32[]{:S(2)}, u32[]{:S(2)}) async-start(f32[16,8,128]{2,1,0:T(8,128)} %get-tuple-element.23), calls=%async_computation | async-start | bytes 131072 | tf_op jit(solution)/shard_map/all_to_all | solution.py:424
  18.2 0.0 copy-done.2
  18.2 2.9 %collective-permute-start = (f32[8,128]{1,0:T(8,128)S(1)}, f32[8,128]{1,0:T(8,128)S(1)}, u32[]{:S(2)}, u32[]{:S(2)}) collective-permute-start(f32[8,128]{1,0:T(8,128)S(1)} %copy-done.2), channel_id=1, source_target_pairs={{0,1},{1,0},{2,3},{3,2},{4,5},{5,4},{6,7},{7,6},{8,9},{9,8},{10,11... | collective-permute-start | bytes 12296 | tf_op jit(solution)/shard_map/ppermute | solution.py:451
  21.1 0.8 %collective-permute-done.beside = f32[8,128]{1,0:T(8,128)S(1)} collective-permute-done((f32[8,128]{1,0:T(8,128)S(1)}, f32[8,128]{1,0:T(8,128)S(1)}, u32[]{:S(2)}, u32[]{:S(2)}) %collective-permute-start) | collective-permute-done | bytes 4128 | tf_op jit(solution)/shard_map/ppermute | solution.py:451
  21.9 4.8 %collective-permute-start.1 = (f32[16,128]{1,0:T(8,128)S(1)}, f32[16,128]{1,0:T(8,128)S(1)}, u32[]{:S(2)}, u32[]{:S(2)}) collective-permute-start(f32[16,128]{1,0:T(8,128)S(1)} %pad_maximum_fusion), channel_id=1, source_target_pairs={{0,2},{1,3},{2,0},{3,1},{4,6},{5,7},{6,4},{7,5},{8,10},{9,11},{10,... | collective-permute-start | bytes 24584 | tf_op jit(solution)/shard_map/ppermute | solution.py:452
  26.7 1.4 %collective-permute-done.1.across = f32[16,128]{1,0:T(8,128)S(1)} collective-permute-done((f32[16,128]{1,0:T(8,128)S(1)}, f32[16,128]{1,0:T(8,128)S(1)}, u32[]{:S(2)}, u32[]{:S(2)}) %collective-permute-start.1) | collective-permute-done | bytes 8224 | tf_op jit(solution)/shard_map/ppermute | solution.py:452
  28.1 1.7 %all-to-all-done = f32[16,8,128]{2,1,0:T(8,128)S(1)} async-done(((f32[16,8,128]{2,1,0:T(8,128)}), f32[16,8,128]{2,1,0:T(8,128)S(1)}, u32[]{:S(2)}, u32[]{:S(2)}) %all-to-all-start) | async-done | bytes 65568 | tf_op jit(solution)/shard_map/all_to_all | solution.py:424
  29.8 1.0 %shard_map.131 = (f32[8,72,128]{2,1,0:T(8,128)}, f32[72,128]{1,0:T(8,128)S(1)}) custom-call(f32[128,128]{1,0:T(8,128)S(1)} %bitcast.5), custom_call_target="tpu_custom_call" | custom-call | bytes 400000 | tf_op jit(solution)/shard_map/pallas_call | solution.py:410
  30.8 5.0 %all-to-all-start.1 = ((f32[8,72,128]{2,1,0:T(8,128)}), f32[8,72,128]{2,1,0:T(8,128)S(1)}, u32[]{:S(2)}, u32[]{:S(2)}) async-start(f32[8,72,128]{2,1,0:T(8,128)} %get-tuple-element.31), calls=%async_computation.1 | async-start | bytes 589824 | tf_op jit(solution)/shard_map/all_to_all | solution.py:424
  35.8 0.0 copy-start.3
  35.8 0.0 copy-start.5
  35.8 1.7 %shard_map.132.early = f32[8,256]{1,0:T(8,128)S(1)} custom-call(f32[8,128]{1,0:T(8,128)S(1)} %copy-done.2, f32[8,128]{1,0:T(8,128)S(1)} %collective-permute-done.beside, f32[16,128]{1,0:T(8,128)S(1)} %collective-permute-done.1.across, f32[72,128]{1,0:T(8,128)S(1)} %get-tuple-element.27.mine), custom_call_target="tpu_custom_call" | custom-call | flops 10000000 | bytes 400000 | tf_op jit(solution)/shard_map/pallas_call | solution.py:410
  37.5 0.0 copy-done
  37.5 0.0 copy-done.3
  37.5 2.3 %shard_map.133 = (f32[3,512]{1,0:T(4,128)S(1)}, f32[3,64]{1,0:T(4,128)S(1)}) custom-call(f32[3,512]{1,0:T(4,128)S(1)} %copy-done, f32[1,512]{1,0:T(1,128)S(1)} %bitcast.7, f32[8,128]{1,0:T(8,128)S(1)} %copy-done.2, f32[8,128]{1,0:T(8,128)S(1)} %copy-done.5, f32[72,128]{1,0:T(8,128)S(1)} %get-tuple-element.27.mine), custom_call_target="tpu_custom_call" | custom-call | flops 15000000 | bytes 400000 | tf_op jit(solution)/shard_map/pallas_call | solution.py:410
  39.8 1.9 %all-to-all-done.1.stars = f32[8,72,128]{2,1,0:T(8,128)S(1)} async-done(((f32[8,72,128]{2,1,0:T(8,128)}), f32[8,72,128]{2,1,0:T(8,128)S(1)}, u32[]{:S(2)}, u32[]{:S(2)}) %all-to-all-start.1) | async-done | bytes 294944 | tf_op jit(solution)/shard_map/all_to_all | solution.py:424
  41.8 8.0 %shard_map.135 = f32[4,8,128]{2,1,0:T(8,128)} custom-call(f32[8,128]{1,0:T(8,128)S(1)} %copy-done.2, f32[8,128]{1,0:T(8,128)S(1)} %collective-permute-done.beside, f32[16,128]{1,0:T(8,128)S(1)} %collective-permute-done.1.across, f32[8,256]{1,0:T(8,128)S(1)} %shard_map.132.early, f32[8,72,128]{2,1,0:T(8,128)S(1)} %all-to-all-done.1.stars), custom_call_target="tpu_custom_call" | custom-call | flops 70000000 | bytes 400000 | tf_op jit(solution)/shard_map/pallas_call | solution.py:410
  49.8 7.8 %all-to-all-start.2 = ((f32[4,8,128]{2,1,0:T(8,128)}), f32[4,8,128]{2,1,0:T(8,128)S(1)}, u32[]{:S(2)}, u32[]{:S(2)}) async-start(f32[4,8,128]{2,1,0:T(8,128)} %shard_map.135), calls=%async_computation.2 | async-start | bytes 32768 | tf_op jit(solution)/shard_map/all_to_all | solution.py:424
  57.6 0.0 copy-done.6
  57.6 6.8 %shard_map.134 = (f32[3,512]{1,0:T(4,128)}, f32[3,64]{1,0:T(4,128)S(1)}) custom-call(s32[4,8]{1,0:T(4,128)S(1)} %copy-done.6, f32[3,512]{1,0:T(4,128)S(1)} %copy-done, f32[3,512]{1,0:T(4,128)S(1)} %copy-done.4, f32[8,72,128]{2,1,0:T(8,128)S(1)} %all-to-all-done.1.stars, f32[8,128]{1,0:T(8,128)S(1)} %copy-done.2, f32[3,512]{1,0:T(4,128)S(1)} %get-tuple-element.33.early_gal, ...), custom_call_target="tpu_custom_call" | custom-call | flops 50000000 | bytes 400000 | tf_op jit(solution)/shard_map/pallas_call | solution.py:410
  64.3 0.0 all-to-all-done.2.parts
  64.3 0.6 shard_map.136
  (8 shorter events, 0.0 us)
Async XLA Ops:
  2.5 15.8 %copy-start.2 = (f32[8,128]{1,0:T(8,128)S(1)}, f32[8,128]{1,0:T(8,128)}, u32[]{:S(2)}) copy-start(f32[8,128]{1,0:T(8,128)} %get-tuple-element.22.own) | copy-start | bytes 12292
  2.5 27.3 %all-to-all-start = ((f32[16,8,128]{2,1,0:T(8,128)}), f32[16,8,128]{2,1,0:T(8,128)S(1)}, u32[]{:S(2)}, u32[]{:S(2)}) async-start(f32[16,8,128]{2,1,0:T(8,128)} %get-tuple-element.23), calls=%async_computation | async-start | bytes 131072 | tf_op jit(solution)/shard_map/all_to_all | solution.py:424
  18.2 3.7 %collective-permute-start = (f32[8,128]{1,0:T(8,128)S(1)}, f32[8,128]{1,0:T(8,128)S(1)}, u32[]{:S(2)}, u32[]{:S(2)}) collective-permute-start(f32[8,128]{1,0:T(8,128)S(1)} %copy-done.2), channel_id=1, source_target_pairs={{0,1},{1,0},{2,3},{3,2},{4,5},{5,4},{6,7},{7,6},{8,9},{9,8},{10,11... | collective-permute-start | bytes 12296 | tf_op jit(solution)/shard_map/ppermute | solution.py:451
  21.9 6.2 %collective-permute-start.1 = (f32[16,128]{1,0:T(8,128)S(1)}, f32[16,128]{1,0:T(8,128)S(1)}, u32[]{:S(2)}, u32[]{:S(2)}) collective-permute-start(f32[16,128]{1,0:T(8,128)S(1)} %pad_maximum_fusion), channel_id=1, source_target_pairs={{0,2},{1,3},{2,0},{3,1},{4,6},{5,7},{6,4},{7,5},{8,10},{9,11},{10,... | collective-permute-start | bytes 24584 | tf_op jit(solution)/shard_map/ppermute | solution.py:452
  30.8 11.0 %all-to-all-start.1 = ((f32[8,72,128]{2,1,0:T(8,128)}), f32[8,72,128]{2,1,0:T(8,128)S(1)}, u32[]{:S(2)}, u32[]{:S(2)}) async-start(f32[8,72,128]{2,1,0:T(8,128)} %get-tuple-element.31), calls=%async_computation.1 | async-start | bytes 589824 | tf_op jit(solution)/shard_map/all_to_all | solution.py:424
  35.8 1.7 %copy-start = (f32[3,512]{1,0:T(4,128)S(1)}, f32[3,512]{1,0:T(4,128)}, u32[]{:S(2)}) copy-start(f32[3,512]{1,0:T(4,128)} %gpos.3) | copy-start | bytes 18436
  35.8 1.7 %copy-start.3 = (f32[512]{0:T(512)S(1)}, f32[512]{0:T(512)}, u32[]{:S(2)}) copy-start(f32[512]{0:T(512)} %param.18) | copy-start | bytes 6148
  35.8 1.7 %copy-start.5 = (f32[8,128]{1,0:T(8,128)S(1)}, f32[8,128]{1,0:T(8,128)}, u32[]{:S(2)}) copy-start(f32[8,128]{1,0:T(8,128)} %get-tuple-element.28.cells) | copy-start | bytes 12292
  49.8 7.8 %copy-start.4 = (f32[3,512]{1,0:T(4,128)S(1)}, f32[3,512]{1,0:T(4,128)}, u32[]{:S(2)}) copy-start(f32[3,512]{1,0:T(4,128)} %gvel.1) | copy-start | bytes 18436
  49.8 7.8 %copy-start.6 = (s32[4,8]{1,0:T(4,128)S(1)}, s32[4,8]{1,0:T(4,128)}, u32[]{:S(2)}) copy-start(s32[4,8]{1,0:T(4,128)} %leaf_ref.1) | copy-start | bytes 388
  49.8 14.6 %all-to-all-start.2 = ((f32[4,8,128]{2,1,0:T(8,128)}), f32[4,8,128]{2,1,0:T(8,128)S(1)}, u32[]{:S(2)}, u32[]{:S(2)}) async-start(f32[4,8,128]{2,1,0:T(8,128)} %shard_map.135), calls=%async_computation.2 | async-start | bytes 32768 | tf_op jit(solution)/shard_map/all_to_all | solution.py:424
  57.6 6.8 %copy-start.1 = (f32[4,3,64]{2,1,0:T(4,128)S(1)}, f32[4,3,64]{2,1,0:T(4,128)}, u32[]{:S(2)}) copy-start(f32[4,3,64]{2,1,0:T(4,128)} %get-tuple-element.36.state) | copy-start | bytes 9220

commit v7 on v6

--- a/solution.py
+++ b/solution.py
@@ -179,7 +179,7 @@
     return jnp.concatenate([ref[half, pl.ds(at, 8), :] for half in range(2)], axis=1)
 
 
-def hermite_partial(own, beside, across, chunks, table, slots, here, main, drag):
+def hermite_partial(own, beside, across, chunks, table, slots, here, main, drag, spread):
     n_targets = N_NARROW * STARS
     x, y, z, u, v, w, m = [star_plane(chunks, c) for c in range(7)]
     product = m * (x * u + y * v + z * w)
@@ -196,12 +196,13 @@
     p = jnp.concatenate(rows[0:3], axis=0)
     q = jnp.concatenate(rows[3:6], axis=0)
     own_product = jnp.sum(p * q, axis=0, keepdims=True)
-    slots[...] = target_slots(
-        jnp.concatenate([-q, -p, own_product, jnp.ones((1, n_targets), F32)], axis=0)
-    )
-    turned = jnp.transpose(jnp.concatenate([p, jnp.zeros((5, n_targets), F32)], axis=0))
-    for c in range(3):
-        here[c] = jnp.broadcast_to(turned[:, c : c + 1], (n_targets, LANES))
+    if spread:
+        slots[...] = target_slots(
+            jnp.concatenate([-q, -p, own_product, jnp.ones((1, n_targets), F32)], axis=0)
+        )
+        turned = jnp.transpose(jnp.concatenate([p, jnp.zeros((5, n_targets), F32)], axis=0))
+        for c in range(3):
+            here[c] = jnp.broadcast_to(turned[:, c : c + 1], (n_targets, LANES))
     main[...] = jnp.zeros(main.shape, F32)
     drag[...] = jnp.zeros(drag.shape, F32)
 
@@ -230,12 +231,13 @@
     return both
 
 
-def early_hermite_kernel(own, beside, across, mine, out, *scratch):
-    out[...] = hermite_partial(own, beside, across, [mine], *scratch)
-
-
-def hermite_kernel(own, beside, across, early, stars, out, *scratch):
-    both = early[...] + hermite_partial(own, beside, across, other_chunks(stars), *scratch)
+def early_hermite_kernel(own, beside, across, mine, out, slots, here, table, main, drag):
+    out[...] = hermite_partial(own, beside, across, [mine], table, slots, here, main, drag, True)
+
+
+def hermite_kernel(own, beside, across, early, slots, here, stars, out, table, main, drag):
+    chunks = other_chunks(stars)
+    both = early[...] + hermite_partial(own, beside, across, chunks, table, slots, here, main, drag, False)
     me = lax.axis_index(NARROW)
     for n in range(N_NARROW):
         owner = me ^ n
@@ -348,7 +350,7 @@
     return jnp.concatenate([row_sums(part) for part in res], axis=0)
 
 
-def early_pull_kernel(gpos, gmass, own, cells, mine, gal_out, cell_out, table, here, total):
+def early_pull_kernel(gpos, gmass, own, cells, mine, gal_out, cell_out, here, table, total):
     table[...] = jnp.zeros(table.shape, F32)
     cell_table([mine], table)
     body_table(gpos, gmass, table)
@@ -361,14 +363,13 @@
 
 
 def pull_kernel(
-    leaf_ref, gpos, gvel, stars, own, early_gal, early_cell, gal_out, cell_out, table, splanes, here, total
+    leaf_ref, gpos, gvel, stars, own, early_gal, early_cell, here, gal_out, cell_out, table, splanes, total
 ):
     table[...] = jnp.zeros(table.shape, F32)
     splanes[...] = jnp.zeros(splanes.shape, F32)
     others = other_chunks(stars)
     cell_table(others, table)
     star_table(leaf_ref, others + [stars.at[lax.axis_index(XY)]], table, splanes)
-    spread_bodies(gpos, here)
     total[...] = jnp.zeros(total.shape, F32)
     pull_all_bodies(table, CELL_BLOCKS, CELL_BLOCKS, here, total)
     for leaf in range(4):
@@ -456,38 +457,41 @@
     )
     stars = exchange(onward, XY)
     n_targets = N_NARROW * STARS
-    body_scratch = [((3, 4 * LEAF, LANES), F32), ((32, 4 * LEAF), F32)]
-    early_gal, early_cell = call(
+    body_total = ((32, 4 * LEAF), F32)
+    early_gal, early_cell, bodies = call(
         early_pull_kernel,
-        (shape(3, 4 * LEAF), shape(3, STARS)),
-        [((2, 8 * (EARLY_BLOCKS + 8), LANES), F32), *body_scratch],
+        (shape(3, 4 * LEAF), shape(3, STARS), shape(3, 4 * LEAF, LANES)),
+        [((2, 8 * (EARLY_BLOCKS + 8), LANES), F32), body_total],
         work=15_000_000,
     )(gal_pos, masses, own, cells, mine)
 
     def hermite_scratch(blocks):
         return [
             ((2, 16 * (blocks + 4), LANES), F32),
-            ((n_targets, 64), BF16),
-            ((3, n_targets, LANES), F32),
             ((32, n_targets), F32),
             ((3, n_targets, LANES), F32),
         ]
 
-    early = call(early_hermite_kernel, shape(8, n_targets), hermite_scratch(4), work=10_000_000)(
+    early_shapes = (
+        shape(8, n_targets),
+        jax.ShapeDtypeStruct((n_targets, 64), BF16),
+        shape(3, n_targets, LANES),
+    )
+    early, slots, targets = call(early_hermite_kernel, early_shapes, hermite_scratch(4), work=10_000_000)(
         own, beside, across, mine
     )
     early, early_gal, early_cell, stars = lax.optimization_barrier((early, early_gal, early_cell, stars))
     partial = call(hermite_kernel, shape(N_NARROW, 8, LANES), hermite_scratch(28), work=70_000_000)(
-        own, beside, across, early, stars
+        own, beside, across, early, slots, targets, stars
     )
     shared = exchange(partial, NARROW)
     gal_vel_new, cell_acc = call(
         pull_kernel,
         (shape(3, 4 * LEAF), shape(3, STARS)),
-        [((2, 8 * BLOCKS, LANES), F32), ((64 * 8, LANES), F32), *body_scratch],
+        [((2, 8 * BLOCKS, LANES), F32), ((64 * 8, LANES), F32), body_total],
         scalars=1,
         work=50_000_000,
-    )(star_leaf, gal_pos, gal_vel, stars, own, early_gal, early_cell)
+    )(star_leaf, gal_pos, gal_vel, stars, own, early_gal, early_cell, bodies)
     star_pos_new, star_vel_new = call(correct_kernel, (shape(3, STARS), shape(3, STARS)))(
         state, shared, cell_acc
     )

time: 65.4 us -> 65.2 us (level)
  transfers between devices with their start and end apart: 5 -> 5, of which waited for: 4 -> 4; matrix products, arithmetic and copies ran while one was open for 0% -> 0% of each run, Pallas kernels for 17% -> 16%
where the time goes in v7:
time: 65.2 us; the launch traced here: 64.7 us
  starting transfers between devices  36.3 us (56%)
  Pallas kernels  21.9 us (34%)
  waiting for transfers between devices  5.77 us (9%)
  between operations  0.74 us (1%)
    all_to_all x3, starting transfers between devices, exchange(): return lax.all_to_all(x, axis, split_axis=0, concat_axis=0, tiled=True)  28.6 us
    pallas_call x7, Pallas kernels, run(): pl.pallas_call(kernel, out_shape=out_shape, in_specs=[pl.BlockSpec(memory...  21.9 us
    ppermute x1, starting transfers between devices, body(): lax.ppermute(jnp.concatenate([own, beside]), NARROW, [(n, n ^ 2) for n in...  4.81 us
    all_to_all x3, waiting for transfers between devices, exchange(): return lax.all_to_all(x, axis, split_axis=0, concat_axis=0, tiled=True)  3.6 us
    ppermute x1, starting transfers between devices, body(): beside = lax.ppermute(own, NARROW, [(n, n ^ 1) for n in range(N_NARROW)])  2.86 us
    ppermute x1, waiting for transfers between devices, body(): lax.ppermute(jnp.concatenate([own, beside]), NARROW, [(n, n ^ 2) for n in...  1.36 us
  transfers between devices with their start and end apart: 5, of which 4 were waited for; matrix products, arithmetic and copies ran while one was open for 0% of the time, Pallas kernels for 16%

profile of v7, /device:TPU:1, one launch (start us, length us, event | category | flops | bytes accessed | tf_op | source)
XLA Modules:
  0.0 64.7 jit_solution(5654636096419842336)
XLA Ops:
  0.6 1.8 %shard_map.130 = (f32[8,128]{1,0:T(8,128)}, f32[8,128]{1,0:T(8,128)}, f32[16,8,128]{2,1,0:T(8,128)}, f32[4,3,64]{2,1,0:T(4,128)}) custom-call(f32[3,64]{1,0:T(4,128)} %refs_0_.1, f32[3,64]{1,0:T(4,128)} %refs_1_.1, f32[3,64]{1,0:T(4,128)} %refs_2_.1, f32[3,64]{1,0:T(4,128)} %refs_3_.1, f32[1,64]{1,0:T(1,128)} %bitcast.9, f32[3,512]{1,0:T(4,128)} %gpos.3, ...), custom_call_target="tpu_custom_call" | custom-call | bytes 400000 | tf_op jit(solution)/shard_map/pallas_call | solution.py:411
  2.4 0.0 copy-start.2
  2.4 15.8 %all-to-all-start = ((f32[16,8,128]{2,1,0:T(8,128)}), f32[16,8,128]{2,1,0:T(8,128)S(1)}, u32[]{:S(2)}, u32[]{:S(2)}) async-start(f32[16,8,128]{2,1,0:T(8,128)} %get-tuple-element.27), calls=%async_computation | async-start | bytes 131072 | tf_op jit(solution)/shard_map/all_to_all | solution.py:425
  18.2 0.0 copy-done.2
  18.2 2.9 %collective-permute-start = (f32[8,128]{1,0:T(8,128)S(1)}, f32[8,128]{1,0:T(8,128)S(1)}, u32[]{:S(2)}, u32[]{:S(2)}) collective-permute-start(f32[8,128]{1,0:T(8,128)S(1)} %copy-done.2), channel_id=1, source_target_pairs={{0,1},{1,0},{2,3},{3,2},{4,5},{5,4},{6,7},{7,6},{8,9},{9,8},{10,11... | collective-permute-start | bytes 12296 | tf_op jit(solution)/shard_map/ppermute | solution.py:452
  21.1 0.8 %collective-permute-done.beside = f32[8,128]{1,0:T(8,128)S(1)} collective-permute-done((f32[8,128]{1,0:T(8,128)S(1)}, f32[8,128]{1,0:T(8,128)S(1)}, u32[]{:S(2)}, u32[]{:S(2)}) %collective-permute-start) | collective-permute-done | bytes 4128 | tf_op jit(solution)/shard_map/ppermute | solution.py:452
  21.9 4.8 %collective-permute-start.1 = (f32[16,128]{1,0:T(8,128)S(1)}, f32[16,128]{1,0:T(8,128)S(1)}, u32[]{:S(2)}, u32[]{:S(2)}) collective-permute-start(f32[16,128]{1,0:T(8,128)S(1)} %pad_maximum_fusion), channel_id=1, source_target_pairs={{0,2},{1,3},{2,0},{3,1},{4,6},{5,7},{6,4},{7,5},{8,10},{9,11},{10,... | collective-permute-start | bytes 24584 | tf_op jit(solution)/shard_map/ppermute | solution.py:453
  26.7 1.4 %collective-permute-done.1.across = f32[16,128]{1,0:T(8,128)S(1)} collective-permute-done((f32[16,128]{1,0:T(8,128)S(1)}, f32[16,128]{1,0:T(8,128)S(1)}, u32[]{:S(2)}, u32[]{:S(2)}) %collective-permute-start.1) | collective-permute-done | bytes 8224 | tf_op jit(solution)/shard_map/ppermute | solution.py:453
  28.1 1.7 %all-to-all-done = f32[16,8,128]{2,1,0:T(8,128)S(1)} async-done(((f32[16,8,128]{2,1,0:T(8,128)}), f32[16,8,128]{2,1,0:T(8,128)S(1)}, u32[]{:S(2)}, u32[]{:S(2)}) %all-to-all-start) | async-done | bytes 65568 | tf_op jit(solution)/shard_map/all_to_all | solution.py:425
  29.8 1.0 %shard_map.131 = (f32[8,72,128]{2,1,0:T(8,128)}, f32[72,128]{1,0:T(8,128)S(1)}) custom-call(f32[128,128]{1,0:T(8,128)S(1)} %bitcast.5), custom_call_target="tpu_custom_call" | custom-call | bytes 400000 | tf_op jit(solution)/shard_map/pallas_call | solution.py:411
  30.7 5.0 %all-to-all-start.1 = ((f32[8,72,128]{2,1,0:T(8,128)}), f32[8,72,128]{2,1,0:T(8,128)S(1)}, u32[]{:S(2)}, u32[]{:S(2)}) async-start(f32[8,72,128]{2,1,0:T(8,128)} %get-tuple-element.36), calls=%async_computation.1 | async-start | bytes 589824 | tf_op jit(solution)/shard_map/all_to_all | solution.py:425
  35.8 0.0 copy-start.3
  35.8 0.0 copy-start.5
  35.8 1.7 %shard_map.132 = (f32[8,256]{1,0:T(8,128)S(1)}, bf16[256,64]{1,0:T(8,128)(2,1)S(1)}, f32[3,256,128]{2,1,0:T(8,128)S(1)}) custom-call(f32[8,128]{1,0:T(8,128)S(1)} %copy-done.2, f32[8,128]{1,0:T(8,128)S(1)} %collective-permute-done.beside, f32[16,128]{1,0:T(8,128)S(1)} %collective-permute-done.1.across, f32[72,128]{1,0:T(8,128)S(1)} %get-tuple-element.31.mine), custom_call_target="tpu_custom_call" | custom-call | flops 10000000 | bytes 400000 | tf_op jit(solution)/shard_map/pallas_call | solution.py:411
  37.5 0.0 copy-done
  37.5 0.0 copy-done.3
  37.5 0.0 copy-done.5
  37.5 2.3 %shard_map.133 = (f32[3,512]{1,0:T(4,128)S(1)}, f32[3,64]{1,0:T(4,128)S(1)}, f32[3,512,128]{2,1,0:T(8,128)S(1)}) custom-call(f32[3,512]{1,0:T(4,128)S(1)} %copy-done, f32[1,512]{1,0:T(1,128)S(1)} %bitcast.7, f32[8,128]{1,0:T(8,128)S(1)} %copy-done.2, f32[8,128]{1,0:T(8,128)S(1)} %copy-done.5, f32[72,128]{1,0:T(8,128)S(1)} %get-tuple-element.31.mine), custom_call_target="tpu_custom_call" | custom-call | flops 15000000 | bytes 400000 | tf_op jit(solution)/shard_map/pallas_call | solution.py:411
  39.8 1.9 %all-to-all-done.1.stars = f32[8,72,128]{2,1,0:T(8,128)S(1)} async-done(((f32[8,72,128]{2,1,0:T(8,128)}), f32[8,72,128]{2,1,0:T(8,128)S(1)}, u32[]{:S(2)}, u32[]{:S(2)}) %all-to-all-start.1) | async-done | bytes 294944 | tf_op jit(solution)/shard_map/all_to_all | solution.py:425
  41.7 7.9 %shard_map.135 = f32[4,8,128]{2,1,0:T(8,128)} custom-call(f32[8,128]{1,0:T(8,128)S(1)} %copy-done.2, f32[8,128]{1,0:T(8,128)S(1)} %collective-permute-done.beside, f32[16,128]{1,0:T(8,128)S(1)} %collective-permute-done.1.across, f32[8,256]{1,0:T(8,128)S(1)} %get-tuple-element.43.early, bf16[256,64]{1,0:T(8,128)(2,1)S(1)} %get-tuple-element.44.slots, ...), custom_call_target="tpu_custom_call" | custom-call | flops 70000000 | bytes 400000 | tf_op jit(solution)/shard_map/pallas_call | solution.py:411
  49.7 7.8 %all-to-all-start.2 = ((f32[4,8,128]{2,1,0:T(8,128)}), f32[4,8,128]{2,1,0:T(8,128)S(1)}, u32[]{:S(2)}, u32[]{:S(2)}) async-start(f32[4,8,128]{2,1,0:T(8,128)} %shard_map.135), calls=%async_computation.2 | async-start | bytes 32768 | tf_op jit(solution)/shard_map/all_to_all | solution.py:425
  57.5 6.7 %shard_map.134 = (f32[3,512]{1,0:T(4,128)}, f32[3,64]{1,0:T(4,128)S(1)}) custom-call(s32[4,8]{1,0:T(4,128)S(1)} %copy-done.6, f32[3,512]{1,0:T(4,128)S(1)} %copy-done, f32[3,512]{1,0:T(4,128)S(1)} %copy-done.4, f32[8,72,128]{2,1,0:T(8,128)S(1)} %all-to-all-done.1.stars, f32[8,128]{1,0:T(8,128)S(1)} %copy-done.2, f32[3,512]{1,0:T(4,128)S(1)} %get-tuple-element.38.early_gal, ...), custom_call_target="tpu_custom_call" | custom-call | flops 50000000 | bytes 400000 | tf_op jit(solution)/shard_map/pallas_call | solution.py:411
  64.1 0.0 all-to-all-done.2.parts
  64.2 0.6 shard_map.136
  (8 shorter events, 0.0 us)
Async XLA Ops:
  2.4 15.8 %copy-start.2 = (f32[8,128]{1,0:T(8,128)S(1)}, f32[8,128]{1,0:T(8,128)}, u32[]{:S(2)}) copy-start(f32[8,128]{1,0:T(8,128)} %get-tuple-element.26.own) | copy-start | bytes 12292
  2.4 27.3 %all-to-all-start = ((f32[16,8,128]{2,1,0:T(8,128)}), f32[16,8,128]{2,1,0:T(8,128)S(1)}, u32[]{:S(2)}, u32[]{:S(2)}) async-start(f32[16,8,128]{2,1,0:T(8,128)} %get-tuple-element.27), calls=%async_computation | async-start | bytes 131072 | tf_op jit(solution)/shard_map/all_to_all | solution.py:425
  18.2 3.7 %collective-permute-start = (f32[8,128]{1,0:T(8,128)S(1)}, f32[8,128]{1,0:T(8,128)S(1)}, u32[]{:S(2)}, u32[]{:S(2)}) collective-permute-start(f32[8,128]{1,0:T(8,128)S(1)} %copy-done.2), channel_id=1, source_target_pairs={{0,1},{1,0},{2,3},{3,2},{4,5},{5,4},{6,7},{7,6},{8,9},{9,8},{10,11... | collective-permute-start | bytes 12296 | tf_op jit(solution)/shard_map/ppermute | solution.py:452
  21.9 6.2 %collective-permute-start.1 = (f32[16,128]{1,0:T(8,128)S(1)}, f32[16,128]{1,0:T(8,128)S(1)}, u32[]{:S(2)}, u32[]{:S(2)}) collective-permute-start(f32[16,128]{1,0:T(8,128)S(1)} %pad_maximum_fusion), channel_id=1, source_target_pairs={{0,2},{1,3},{2,0},{3,1},{4,6},{5,7},{6,4},{7,5},{8,10},{9,11},{10,... | collective-permute-start | bytes 24584 | tf_op jit(solution)/shard_map/ppermute | solution.py:453
  30.7 11.0 %all-to-all-start.1 = ((f32[8,72,128]{2,1,0:T(8,128)}), f32[8,72,128]{2,1,0:T(8,128)S(1)}, u32[]{:S(2)}, u32[]{:S(2)}) async-start(f32[8,72,128]{2,1,0:T(8,128)} %get-tuple-element.36), calls=%async_computation.1 | async-start | bytes 589824 | tf_op jit(solution)/shard_map/all_to_all | solution.py:425
  35.8 1.7 %copy-start = (f32[3,512]{1,0:T(4,128)S(1)}, f32[3,512]{1,0:T(4,128)}, u32[]{:S(2)}) copy-start(f32[3,512]{1,0:T(4,128)} %gpos.3) | copy-start | bytes 18436
  35.8 1.7 %copy-start.3 = (f32[512]{0:T(512)S(1)}, f32[512]{0:T(512)}, u32[]{:S(2)}) copy-start(f32[512]{0:T(512)} %param.18) | copy-start | bytes 6148
  35.8 1.7 %copy-start.5 = (f32[8,128]{1,0:T(8,128)S(1)}, f32[8,128]{1,0:T(8,128)}, u32[]{:S(2)}) copy-start(f32[8,128]{1,0:T(8,128)} %get-tuple-element.33.cells) | copy-start | bytes 12292
  49.6 7.8 %copy-start.4 = (f32[3,512]{1,0:T(4,128)S(1)}, f32[3,512]{1,0:T(4,128)}, u32[]{:S(2)}) copy-start(f32[3,512]{1,0:T(4,128)} %gvel.1) | copy-start | bytes 18436
  49.7 7.8 %copy-start.6 = (s32[4,8]{1,0:T(4,128)S(1)}, s32[4,8]{1,0:T(4,128)}, u32[]{:S(2)}) copy-start(s32[4,8]{1,0:T(4,128)} %leaf_ref.1) | copy-start | bytes 388
  49.7 14.5 %all-to-all-start.2 = ((f32[4,8,128]{2,1,0:T(8,128)}), f32[4,8,128]{2,1,0:T(8,128)S(1)}, u32[]{:S(2)}, u32[]{:S(2)}) async-start(f32[4,8,128]{2,1,0:T(8,128)} %shard_map.135), calls=%async_computation.2 | async-start | bytes 32768 | tf_op jit(solution)/shard_map/all_to_all | solution.py:425
  57.5 6.7 %copy-start.1 = (f32[4,3,64]{2,1,0:T(4,128)S(1)}, f32[4,3,64]{2,1,0:T(4,128)}, u32[]{:S(2)}) copy-start(f32[4,3,64]{2,1,0:T(4,128)} %get-tuple-element.42.state) | copy-start | bytes 9220
